TPU v7x, 32 devices: a whole 2x2x4 slice. The times are simulated.
32 devices in a mesh: dp: 8 (over z, x), space: 4 (over y, core).
Axes of the slice: x: 2, y: 2, z: 4, core: 2. Of those that a mesh axis runs over, the one named last changes fastest.
Arguments:
- branch_zero: float32 [16, 128, 4096], P('dp', 'space'), may hold values from -6 to 6
- branch_one: float32 [16, 64, 4096], P('dp', 'space'), may hold values from -6 to 6
- branch_two: float32 [16, 32, 4096], P('dp', 'space'), may hold values from -6 to 6
- branch_three: float32 [16, 16, 4096], P('dp', 'space'), may hold values from -6 to 6
- convs_zero: float32 [18432], P(('dp', 'space')), may hold values from -0.375 to 0.375
- convs_one: float32 [73728], P(('dp', 'space')), may hold values from -0.25 to 0.25
- convs_two: float32 [294912], P(('dp', 'space')), may hold values from -0.1875 to 0.1875
- convs_three: float32 [1179648], P(('dp', 'space')), may hold values from -0.125 to 0.125
- unite_one: float32 [2048], P(('dp', 'space')), may hold values from -0.75 to 0.75
- unite_two: float32 [4096], P(('dp', 'space')), may hold values from -0.5 to 0.5
- unite_three: float32 [8192], P(('dp', 'space')), may hold values from -0.375 to 0.375
- norm_gain: float32 [1056], replicated, may hold values from 0.1 to 1.9
- norm_shift: float32 [1056], replicated, may hold values from -3 to 3
- head_weight: float32 [32, 17], replicated, may hold values from -1 to 1
- head_bias: float32 [17], replicated, may hold values from -3 to 3
- targets: float32 [16, 17, 128, 128], P('dp', None, 'space'), may hold values from -6 to 6
- crowd_mask: int32 [16, 128, 128], P('dp', 'space'), may hold values 0 or 1
- person_count: int32 [16], P('dp'), may hold values from 1 to 8
- flip_order: int32 [17], replicated, may hold values from 0 to 16, each once
Outputs:
- loss_value: float32 [], replicated
- heat_mean: float32 [16, 17, 128, 128], P('dp', None, 'space')
- grad_branch_zero: float32 [16, 128, 4096], P('dp', 'space')
- grad_branch_one: float32 [16, 64, 4096], P('dp', 'space')
- grad_branch_two: float32 [16, 32, 4096], P('dp', 'space')
- grad_branch_three: float32 [16, 16, 4096], P('dp', 'space')
- grad_convs_zero: float32 [18432], P(('dp', 'space'))
- grad_convs_one: float32 [73728], P(('dp', 'space'))
- grad_convs_two: float32 [294912], P(('dp', 'space'))
- grad_convs_three: float32 [1179648], P(('dp', 'space'))
- grad_unite_one: float32 [2048], P(('dp', 'space'))
- grad_unite_two: float32 [4096], P(('dp', 'space'))
- grad_unite_three: float32 [8192], P(('dp', 'space'))
- grad_norm_gain: float32 [1056], replicated
- grad_norm_shift: float32 [1056], replicated
- grad_head_weight: float32 [32, 17], replicated
- grad_head_bias: float32 [17], replicated
Inputs may be any that keep to these rules, and one draw needn't show every extreme that they name: flip_order is a permutation of the 17 joints.
All inputs are finite; a program needn't handle non-finite values. No bound on the sum of `crowd_mask` on one device may be relied on, other than what follows from the above.
Results may differ from a plain program's by a relative error of at most 0.0003.
Values sent between devices are 32-bit elements; how exact they have to be, the bound alone decides.
No kernel may reach another device: no remote copies, remote signals or barrier semaphores. Data moves between devices by JAX's collectives and lax.ppermute only.
A program may use at most 256 MiB of HBM per device.

v0:
```python
import functools

import jax
import jax.numpy as jnp
import numpy as np
from jax import lax
from jax.experimental import pallas as pl
from jax.experimental.pallas import tpu as pltpu
from jax.sharding import PartitionSpec as P

C0 = 32
CHANNELS = (32, 64, 128, 256)
SIDES = (128, 128, 256, 512)
AXES = ("dp", "space")
epsilon = 1e-05
f32 = jnp.float32
high = lax.Precision.HIGH


def dot_nn(left, right):
    return lax.dot_general(left, right, (((1,), (0,)), ((), ())), precision=high, preferred_element_type=f32)


def dot_nt(left, right):
    return lax.dot_general(left, right, (((1,), (1,)), ((), ())), precision=high, preferred_element_type=f32)


def dot_tn(left, right):
    return lax.dot_general(left, right, (((0,), (0,)), ((), ())), precision=high, preferred_element_type=f32)


def sigmoid(value):
    return 1.0 / (1.0 + jnp.exp(-value))


def silu(value):
    return value * sigmoid(value)


def silu_slope(value):
    sigma = sigmoid(value)
    return sigma * (1.0 + value * (1.0 - sigma))


def fold(row, channels):
    step = channels
    while step < 256:
        row = row + pltpu.roll(row, step, 1)
        step = 2 * step
    return row


def column_sum(value):
    return jnp.sum(value, axis=0, keepdims=True)


def moments(sums, channels, count):
    mean = fold(sums[0:1], channels) / count
    square = fold(sums[1:2], channels) / count
    return mean, lax.rsqrt(square - mean * mean + epsilon)


def affine(stats, gain, shift):
    scale = stats[1] * gain
    return scale, shift - stats[0] * scale


def load_rows(ref, first, count):
    lanes = ref.shape[2]
    return ref[:, first * 16 : (first + count) * 16, :].reshape(2 * count * 16, lanes)


def group_index(rows):
    return lax.broadcasted_iota(jnp.int32, (rows, 128), 0) % 16


def side_columns(value, channels):
    rows = value.shape[0]
    group = group_index(rows)
    lane = lax.broadcasted_iota(jnp.int32, (rows, 128), 1)

    def before(part):
        return jnp.where(group == 0, 0.0, pltpu.roll(part, 1, 0))

    def after(part):
        return jnp.where(group == 15, 0.0, pltpu.roll(part, rows - 1, 0))

    low, upper = value[:, :128], value[:, 128:]
    if channels == 256:
        return jnp.concatenate([before(low), before(upper), after(low), after(upper)], axis=1)
    if channels == 128:
        return jnp.concatenate([before(upper), after(low)], axis=1)
    return jnp.where(
        lane < channels, after(low), jnp.where(lane >= 128 - channels, before(upper), 0.0)
    )


def build_sides(source, side, channels):
    rows = source.shape[1]
    for image in range(2):
        side[image] = side_columns(source[image], channels)


def patches(source, side, count):
    parts = []
    for tap_row in range(3):
        parts.append(load_rows(source, tap_row, count))
        parts.append(load_rows(side, tap_row, count))
    return jnp.concatenate(parts, axis=1)


def build_band(band, tap, branch, offset):
    channels = CHANNELS[branch]
    groups = 256 // channels
    side = SIDES[branch]
    height = 256 + side
    if channels < 256:
        band[:, offset : offset + 256] = jnp.zeros((3 * height, 256), f32)
    for tap_row in range(3):
        base = tap_row * height
        for tap_col in range(3):
            matrix = tap(tap_row, tap_col)
            for out in range(groups):
                place = out + tap_col - 1
                if place < 0:
                    row = base + 256 + (0 if channels >= 128 else 128 - channels)
                elif place >= groups:
                    row = base + 256 + (side // 2 if channels >= 128 else 0)
                else:
                    row = base + place * channels
                start = offset + out * channels
                band[row : row + channels, start : start + channels] = matrix


def collect_band(product, branch, emit):
    channels = CHANNELS[branch]
    groups = 256 // channels
    side = SIDES[branch]
    height = 256 + side
    for tap_row in range(3):
        base = tap_row * height
        for tap_col in range(3):
            total = None
            for out in range(groups):
                place = out + tap_col - 1
                if place < 0:
                    row = base + 256 + (0 if channels >= 128 else 128 - channels)
                elif place >= groups:
                    row = base + 256 + (side // 2 if channels >= 128 else 0)
                else:
                    row = base + place * channels
                start = out * channels
                if channels >= 128:
                    block = product[row : row + channels, start : start + channels]
                else:
                    tile = start // 128 * 128
                    block = product[row : row + channels, tile : tile + 128]
                    inner = start - tile
                    if inner:
                        block = pltpu.roll(block, 128 - inner, 1)
                total = block if total is None else total + block
            emit(tap_row, tap_col, total[:, :channels])


def tap_reader(ref, branch):
    channels = CHANNELS[branch]
    if channels == 256:

        def tap(tap_row, tap_col):
            first = (3 * tap_row + tap_col) * 512
            return jnp.concatenate(
                [ref[pl.ds(first, 256, stride=2), :], ref[pl.ds(first + 1, 256, stride=2), :]],
                axis=1,
            )

        return tap

    def tap(tap_row, tap_col):
        first = (3 * tap_row + tap_col) * channels
        return ref[first : first + channels, :]

    return tap


def tap_writer(ref, branch):
    channels = CHANNELS[branch]

    def emit(tap_row, tap_col, value):
        place = 3 * tap_row + tap_col
        if channels == 256:
            ref[pl.ds(place * 512, 256, stride=2), :] = value[:, :128]
            ref[pl.ds(place * 512 + 1, 256, stride=2), :] = value[:, 128:]
        else:
            ref[place * channels : (place + 1) * channels, :] = value

    return emit


SPLIT = 200
SHARD = 392
ROWS_THREE, ROWS_TWO, ROWS_ONE = 288, 72, 18
PER_ZERO, PER_UNITE = 18, (2, 4, 8)
GATHER_ORDER = ((2, 4, 8), (4, 2, 8))
SCATTER_ORDER = ((4, 2, 8), (2, 4, 8))
TAPS_OUT = ((4608, 128), (1152, 128), (576, 64), (288, 32), (32, 32), (64, 32), (128, 32))
PACK_SCRATCH = ((16, 24, 128), (16, 8, 128), (288, 128))
STAGE = ((4608, 128), (1152, 128), (576, 64), (288, 32), (512, 32))


def partner(me, core, place, order):
    bits = sum(bit for i, bit in enumerate(order) if place >> (2 - i) & 1)
    return me ^ (bits + core)


def unpack_taps(me, packs, taps, scratch):
    three, two, one, zero = taps[:4]
    part_one, part_zero, flat_one = scratch
    for core in range(2):
        upper, lower = packs[core], packs[2 + core]
        for place in range(8):
            device = partner(me, core, place, GATHER_ORDER[0])
            start = pl.multiple_of(device * ROWS_THREE, 8)
            three[pl.ds(start, SPLIT), :] = upper[place]
            device = partner(me, core, place, GATHER_ORDER[1])
            rest = ROWS_THREE - SPLIT
            start = pl.multiple_of(device * ROWS_THREE + SPLIT, 8)
            three[pl.ds(start, rest), :] = lower[place, 0:rest]
            start = pl.multiple_of(device * ROWS_TWO, 8)
            two[pl.ds(start, ROWS_TWO), :] = lower[place, rest : rest + ROWS_TWO]
            part_one[device] = lower[place, rest + ROWS_TWO : rest + ROWS_TWO + 24]
            part_zero[device] = lower[place, rest + ROWS_TWO + 24 :]
    for device in range(16):
        flat_one[device * ROWS_ONE : (device + 1) * ROWS_ONE, :] = part_one[device, 0:ROWS_ONE]
    one[...] = flat_one[...].reshape(one.shape)
    narrow = part_zero[...].reshape(128, 128).reshape(512, 32)
    for device in range(16):
        first = device * 32
        for ref, height in zip(taps[3:7], (PER_ZERO, *PER_UNITE)):
            ref[device * height : (device + 1) * height, :] = narrow[first : first + height]
            first += height


def pack_grads(me, stage, unite_grads, packs, scratch):
    three, two, one, zero, narrow = stage
    part_one, part_zero, flat_one = scratch
    flat_one[...] = one[...].reshape(flat_one.shape)
    for device in range(16):
        part_one[device, 0:ROWS_ONE] = flat_one[device * ROWS_ONE : (device + 1) * ROWS_ONE, :]
        part_one[device, ROWS_ONE:24] = jnp.zeros((24 - ROWS_ONE, 128), f32)
        first = device * 32
        for ref, height in zip((zero, *unite_grads), (PER_ZERO, *PER_UNITE)):
            narrow[first : first + height, :] = ref[device * height : (device + 1) * height, :]
            first += height
    part_zero[...] = narrow[...].reshape(128, 128).reshape(16, 8, 128)
    for core in range(2):
        upper, lower = packs[core], packs[2 + core]
        for place in range(8):
            device = partner(me, core, place, SCATTER_ORDER[0])
            start = pl.multiple_of(device * ROWS_THREE, 8)
            upper[place] = three[pl.ds(start, SPLIT), :]
            device = partner(me, core, place, SCATTER_ORDER[1])
            rest = ROWS_THREE - SPLIT
            start = pl.multiple_of(device * ROWS_THREE + SPLIT, 8)
            lower[place, 0:rest] = three[pl.ds(start, rest), :]
            start = pl.multiple_of(device * ROWS_TWO, 8)
            lower[place, rest : rest + ROWS_TWO] = two[pl.ds(start, ROWS_TWO), :]
            lower[place, rest + ROWS_TWO : rest + ROWS_TWO + 24] = part_one[device]
            lower[place, rest + ROWS_TWO + 24 :] = part_zero[device]


PACKS = ((8, SPLIT, 128), (8, SPLIT, 128), (8, SHARD - SPLIT, 128), (8, SHARD - SPLIT, 128))


def mirrored(tap):
    return lambda tap_row, tap_col: tap(tap_row, 2 - tap_col)


def turned(tap):
    return lambda tap_row, tap_col: jnp.transpose(tap(2 - tap_row, 2 - tap_col))


def mask_ends(value, rows, flags):
    place = lax.broadcasted_iota(jnp.int32, value.shape, 0) // 16 % (rows + 2)
    outside = ((place == 0) & (flags[0] == 0)) | ((place == rows + 1) & (flags[1] == 0))
    return jnp.where(outside, 0.0, value)


def mix_matrix(unite, branch):
    channels = CHANNELS[branch]
    groups = 256 // channels
    wide = jnp.concatenate([unite] * 8, axis=1)
    lane = lax.broadcasted_iota(jnp.int32, wide.shape, 1)
    span = 256 // groups
    return jnp.concatenate(
        [jnp.where(lane // span == place, wide, 0.0) for place in range(groups)], axis=0
    )


def split_refs(refs, *counts):
    out, first = [], 0
    for count in counts:
        out.append(refs[first : first + count])
        first += count
    assert first == len(refs)
    return out


class Kept:
    def __init__(self, value):
        self.value = value


def kept(values):
    return [Kept(value) for value in values]


def call(kernel, ins, outs, scratch=(), smem=0, limit=16, cost=1):
    specs = [pl.BlockSpec(memory_space=pltpu.SMEM)] * smem + [
        pl.BlockSpec(memory_space=pltpu.VMEM)
    ] * (len(ins) - smem)
    ins = ins[:smem] + [
        pltpu.with_memory_space_constraint(x.value, pltpu.VMEM)
        if isinstance(x, Kept)
        else pltpu.with_memory_space_constraint(x, pltpu.HBM)
        for x in ins[smem:]
    ]
    shapes = [pltpu.VMEM(x.value, f32) if isinstance(x, Kept) else pltpu.HBM(x, f32) for x in outs]
    results = pl.pallas_call(
        kernel,
        in_specs=specs,
        out_specs=[pl.BlockSpec(memory_space=pltpu.VMEM)] * len(outs),
        out_shape=shapes,
        scratch_shapes=[pltpu.VMEM(shape, f32) for shape in scratch],
        compiler_params=pltpu.CompilerParams(vmem_limit_bytes=limit * 2**20),
        cost_estimate=pl.CostEstimate(
            flops=int(cost * 1.1e9), bytes_accessed=int(cost * 3.0e6), transcendentals=0
        ),
    )(*ins)
    return [Kept(y) if isinstance(x, Kept) else y for x, y in zip(outs, results)]


def band_shape(branch, width):
    return (3 * (256 + SIDES[branch]), width)


def norm_kernel(gain, shift, out):
    for base, ref in ((0, gain), (11, shift)):
        offset = 0
        line = base
        sizes = [channels for channels in CHANNELS for _ in range(2)] + [C0] * 3
        for channels in sizes:
            part = ref[0:1, offset : offset + channels]
            out[line : line + 1, :] = jnp.concatenate([part] * (256 // channels), axis=1)
            offset += channels
            line += 1


def first_kernel(rows, packed, meta, *refs):
    xs, tops, bottoms, packs, tiles, mains, sums, taps, bands, sides, scratch = split_refs(
        refs, 4, 1, 1, 4, 4, 4, 1, 7 * packed, 4, 4, 3 * packed
    )
    sums = sums[0]
    if packed:
        unpack_taps(meta[2], packs, taps, scratch)
    else:
        taps = packs
    for branch in range(4):
        count = rows[branch]
        tile, side, band = tiles[branch], sides[branch], bands[branch]
        for image in range(2):
            for ref, start, first, extent in (
                (tops[0], 2 * branch, 0, 2),
                (xs[branch], 0, 2, count),
                (bottoms[0], 2 * branch, count + 2, 2),
            ):
                tile[image, first * 16 : (first + extent) * 16, :] = ref[
                    image, start : start + extent, :
                ].reshape(extent * 16, 256)
        build_sides(tile, side, CHANNELS[branch])
        build_band(band, tap_reader(taps[3 - branch], branch), branch, 0)
        out = dot_nn(patches(tile, side, count + 2), band[...])
        mains[branch][...] = out.reshape(2, (count + 2) * 16, 256)
        inner = load_rows(mains[branch], 1, count)
        sums[2 * branch : 2 * branch + 1, :] = column_sum(inner)
        sums[2 * branch + 1 : 2 * branch + 2, :] = column_sum(inner * inner)


def first_flip_kernel(rows, meta, *refs):
    tiles, taps, outs, bands, sides = split_refs(refs, 4, 4, 4, 4, 4)
    for branch in range(4):
        count = rows[branch]
        build_sides(tiles[branch], sides[branch], CHANNELS[branch])
        build_band(bands[branch], mirrored(tap_reader(taps[3 - branch], branch)), branch, 0)
        out = dot_nn(patches(tiles[branch], sides[branch], count + 2), bands[branch][...])
        outs[branch][...] = out.reshape(2, (count + 2) * 16, 256)


def fill_hidden(meta, firsts, stat, norms, hidden, branch, count, total):
    stats = moments(stat[2 * branch : 2 * branch + 2, :], CHANNELS[branch], total)
    scale, offset = affine(
        stats,
        norms[2 * branch : 2 * branch + 1, :],
        norms[11 + 2 * branch : 12 + 2 * branch, :],
    )
    value = load_rows(firsts[branch], 0, count + 2) * scale + offset
    value = mask_ends(silu(value), count, meta)
    hidden[branch][...] = value.reshape(2, (count + 2) * 16, 256)


def second_kernel(rows, counts, packed, meta, *refs):
    firsts, stat, norms, packs, outs, sums, taps, hidden, bands, sides, scratch = split_refs(
        refs, 4, 1, 1, 4, 4, 1, 7 * packed, 4, 4, 4, 3 * packed
    )
    sums = sums[0]
    if packed:
        unpack_taps(meta[2], packs, taps, scratch)
    else:
        taps = packs
    for branch in range(4):
        count, channels = rows[branch], CHANNELS[branch]
        fill_hidden(meta, firsts, stat[0], norms[0], hidden, branch, count, counts[branch])
        build_sides(hidden[branch], sides[branch], channels)
        build_band(bands[branch], tap_reader(taps[3 - branch], branch), branch, 0)
        out = dot_nn(patches(hidden[branch], sides[branch], count), bands[branch][...])
        outs[branch][...] = out
        sums[2 * branch : 2 * branch + 1, :] = column_sum(out)
        sums[2 * branch + 1 : 2 * branch + 2, :] = column_sum(out * out)


def second_flip_kernel(rows, counts, meta, *refs):
    firsts, stat, norms, taps, outs, hidden, bands, sides = split_refs(refs, 4, 1, 1, 4, 4, 4, 4, 4)
    for branch in range(4):
        count, channels = rows[branch], CHANNELS[branch]
        fill_hidden(meta, firsts, stat[0], norms[0], hidden, branch, count, counts[branch])
        build_sides(hidden[branch], sides[branch], channels)
        build_band(bands[branch], mirrored(tap_reader(taps[3 - branch], branch)), branch, 0)
        outs[branch][...] = dot_nn(
            patches(hidden[branch], sides[branch], count), bands[branch][...]
        )


def joined(second, tile, stat, norms, branch, count, total):
    stats = moments(stat[2 * branch : 2 * branch + 2, :], CHANNELS[branch], total)
    gain = norms[2 * branch + 1 : 2 * branch + 2, :]
    shift = norms[12 + 2 * branch : 13 + 2 * branch, :]
    scaled = (second - stats[0]) * stats[1]
    return scaled * gain + shift + load_rows(tile, 2, count), scaled, stats


def third_kernel(rows, counts, *refs):
    seconds, tiles, stat, norms, unites, mixes, sums = split_refs(refs, 3, 3, 1, 1, 6, 3, 1)
    stat, norms, sums = stat[0], norms[0], sums[0]
    for level in range(3):
        branch = level + 1
        value, _, _ = joined(
            seconds[level][...], tiles[level], stat, norms, branch, rows[branch], counts[branch]
        )
        unite = jnp.concatenate([unites[level][...], unites[3 + level][...]], axis=0)
        mixed = dot_nn(silu(value), mix_matrix(unite, branch))
        mixes[level][...] = mixed
        sums[2 * level : 2 * level + 1, :] = column_sum(mixed)
        sums[2 * level + 1 : 2 * level + 2, :] = column_sum(mixed * mixed)
    sums[6:8, :] = jnp.zeros((2, 256), f32)


def spread_rows(value, rows, factor):
    value = value.reshape(2 * rows, 1, 16, 256)
    return jnp.broadcast_to(value, (2 * rows, factor, 16, 256)).reshape(2 * rows * factor * 16, 256)


def gather_rows(value, rows, factor):
    value = value.reshape(2 * rows // factor, factor, 16, 256)
    return jnp.sum(value, axis=1).reshape(2 * rows // factor * 16, 256)


def uniting_stats(stat, level, total):
    return moments(stat[2 * level : 2 * level + 2, :], C0, total * 2.0 ** (level + 1))


def united_sum(base, mixes, stat, norms, rows, counts):
    for level in range(3):
        stats = uniting_stats(stat, level, counts[level + 1])
        scale, offset = affine(
            stats, norms[8 + level : 9 + level, :], norms[19 + level : 20 + level, :]
        )
        base = base + spread_rows(mixes[level] * scale + offset, rows[level + 1], 2 ** (level + 1))
    return base


def head_matrix(weight):
    wide = jnp.concatenate([weight] * 8, axis=1)
    lane = lax.broadcasted_iota(jnp.int32, wide.shape, 1)
    return jnp.concatenate([jnp.where(lane // C0 == place, wide, 0.0) for place in range(8)], axis=0)


def loss_kernel(rows, counts, denominator, *refs):
    ins, outs = split_refs(refs, 12, 6)
    second, tile, stat, mix_one, mix_two, mix_three, mix_stat, norms, weight, bias, targets, mask = ins
    heat_out, sum_one, sum_two, sum_three, sums, join_grad = outs
    count = rows[0]
    join, scaled, _ = joined(second[...], tile, stat, norms, 0, count, counts[0])
    mixes = (mix_one[...], mix_two[...], mix_three[...])
    pre = united_sum(silu(join), mixes, mix_stat, norms, rows, counts)
    united = silu(pre)
    head = head_matrix(weight[...])
    heat = dot_nn(united, head) + bias[...]
    heat_out[...] = heat
    error = heat - targets[...]
    weighted = mask[...] * error
    sums[...] = jnp.zeros(sums.shape, f32)
    sums[6:7, :] = column_sum(weighted * error) / denominator
    heat_grad = weighted * (2.0 / denominator)
    sums[7:8, :] = column_sum(heat_grad)
    product = dot_tn(united, heat_grad)
    total = None
    for place in range(8):
        first = place * C0
        tile_first = first // 128 * 128
        block = product[first : first + C0, tile_first : tile_first + 128]
        if first - tile_first:
            block = pltpu.roll(block, 128 - (first - tile_first), 1)
        total = block if total is None else total + block
    sums[16:24, 0:128] = jnp.concatenate(
        [total[8 * part : 8 * part + 8, :C0] for part in range(4)], axis=1
    )
    grad = dot_nt(heat_grad, head) * silu_slope(pre)
    join_part = grad * silu_slope(join)
    join_grad[...] = join_part
    sums[8:9, :] = column_sum(join_part)
    sums[9:10, :] = column_sum(join_part * scaled)
    for level, out in enumerate((sum_one, sum_two, sum_three)):
        part = gather_rows(grad, count, 2 ** (level + 1))
        out[...] = part
        stats = uniting_stats(mix_stat, level, counts[level + 1])
        normed = (mixes[level] - stats[0]) * stats[1]
        sums[2 * level : 2 * level + 1, :] = column_sum(part)
        sums[2 * level + 1 : 2 * level + 2, :] = column_sum(part * normed)


def flip_kernel(rows, counts, *refs):
    seconds, tiles, stat, unites, mix_stat, norms, weight, bias, heat, out = split_refs(
        refs, 4, 4, 1, 6, 1, 1, 1, 1, 1, 1
    )
    stat, norms = stat[0], norms[0]
    mixes = []
    for branch in range(4):
        value, _, _ = joined(
            seconds[branch][...], tiles[branch], stat, norms, branch, rows[branch], counts[branch]
        )
        if branch == 0:
            base = silu(value)
        else:
            unite = jnp.concatenate([unites[branch - 1][...], unites[branch + 2][...]], axis=0)
            mixes.append(dot_nn(silu(value), mix_matrix(unite, branch)))
    pre = united_sum(base, mixes, mix_stat[0], norms, rows, counts)
    back = dot_nn(silu(pre), head_matrix(weight[0][...])) + bias[0][...]
    out[0][...] = 0.5 * (heat[0][...] + back)


def edge_place(branch, image):
    return (2 * branch + image) * 16


def write_edges(first, last, value, branch, count, base):
    for image in range(2):
        place = base + edge_place(branch, image)
        start = image * count * 16
        first[place : place + 16, :] = value[start : start + 16]
        last[place : place + 16, :] = value[start + (count - 1) * 16 : start + count * 16]


def join_kernel(rows, counts, *refs):
    sums_in, mixes, seconds, tiles, join_zero, stat, mix_stat, head_sums, norms, unites, outs = (
        split_refs(refs, 3, 3, 4, 3, 1, 1, 1, 1, 1, 6, 9)
    )
    stat, mix_stat, head_sums, norms = stat[0], mix_stat[0], head_sums[0], norms[0]
    grads, mixer_grads, sums, first, last = outs[0:3], outs[3:6], outs[6], outs[7], outs[8]
    sums[0:2, :] = jnp.zeros((2, 256), f32)
    write_edges(first, last, join_zero[0][...], 0, rows[0], 0)
    write_edges(first, last, seconds[0][...], 0, rows[0], 128)
    for level in range(3):
        branch = level + 1
        channels, count = CHANNELS[branch], rows[branch]
        groups = 256 // channels
        total = counts[branch]
        stats = uniting_stats(mix_stat, level, total)
        gain = norms[8 + level : 9 + level, :]
        shift_sum = fold(head_sums[2 * level : 2 * level + 1, :], C0)
        gain_sum = fold(head_sums[2 * level + 1 : 2 * level + 2, :], C0)
        normed = (mixes[level][...] - stats[0]) * stats[1]
        share = 1.0 / (total * 2.0 ** (level + 1))
        mixed_grad = (gain * stats[1]) * (
            sums_in[level][...] - shift_sum * share - normed * (gain_sum * share)
        )
        value, scaled, _ = joined(
            seconds[branch][...], tiles[level], stat, norms, branch, count, total
        )
        unite = jnp.concatenate([unites[level][...], unites[3 + level][...]], axis=0)
        product = dot_tn(silu(value), mixed_grad)
        mixer = None
        for place in range(8):
            row = place // (8 // groups) * channels
            tile_first = place * C0 // 128 * 128
            block = product[row : row + channels, tile_first : tile_first + 128]
            inner = place * C0 - tile_first
            if inner:
                block = pltpu.roll(block, 128 - inner, 1)
            mixer = block if mixer is None else mixer + block
        mixer_grads[level][...] = mixer[:, :C0]
        grad = dot_nt(mixed_grad, mix_matrix(unite, branch)) * silu_slope(value)
        grads[level][...] = grad
        sums[2 * branch : 2 * branch + 1, :] = column_sum(grad)
        sums[2 * branch + 1 : 2 * branch + 2, :] = column_sum(grad * scaled)
        write_edges(first, last, grad, branch, count, 0)
        write_edges(first, last, seconds[branch][...], branch, count, 128)


def norm_input_grad(grad, scaled, stats, gain, sums, channels, total):
    shift_sum = fold(sums[0:1, :], channels) / total
    gain_sum = fold(sums[1:2, :], channels) / total
    return (gain * stats[1]) * (grad - shift_sum - scaled * gain_sum)


def back_second_kernel(rows, counts, flags, *refs):
    ins, outs, scratch = split_refs(refs, 22, 7, 12)
    grads, seconds, firsts, taps = ins[0:4], ins[4:8], ins[8:12], ins[12:16]
    above, below, stat, stat_sums, first_stat, norms = ins[16:22]
    normed_grads = outs[0:4]
    sums, first, last = outs[4:7]
    wide = scratch[0:4]
    sides = scratch[4:8]
    bands = scratch[8:12]
    for branch in range(4):
        count, channels, total = rows[branch], CHANNELS[branch], counts[branch]
        stats = moments(stat[2 * branch : 2 * branch + 2, :], channels, total)
        gain = norms[2 * branch + 1 : 2 * branch + 2, :]
        shift_sum = fold(stat_sums[2 * branch : 2 * branch + 1, :], channels) / total
        gain_sum = fold(stat_sums[2 * branch + 1 : 2 * branch + 2, :], channels) / total

        def input_grad(grad, value):
            scaled = (value - stats[0]) * stats[1]
            return (gain * stats[1]) * (grad - shift_sum - scaled * gain_sum)

        inner = input_grad(grads[branch][...], seconds[branch][...])
        wide[branch][:, 16 : (count + 1) * 16, :] = inner.reshape(2, count * 16, 256)
        for image in range(2):
            place = edge_place(branch, image)
            for ref, start, flag in ((above, 0, flags[0]), (below, (count + 1) * 16, flags[1])):
                value = input_grad(
                    ref[place : place + 16, :], ref[128 + place : 144 + place, :]
                )
                wide[branch][image, start : start + 16, :] = jnp.where(flag == 0, 0.0, value)
        build_sides(wide[branch], sides[branch], channels)
        build_band(bands[branch], turned(tap_reader(taps[3 - branch], branch)), branch, 0)
        hidden_grad = dot_nn(patches(wide[branch], sides[branch], count), bands[branch][...])
        first_stats = moments(first_stat[2 * branch : 2 * branch + 2, :], channels, total)
        scaled = (load_rows(firsts[branch], 1, count) - first_stats[0]) * first_stats[1]
        value = (
            scaled * norms[2 * branch : 2 * branch + 1, :]
            + norms[11 + 2 * branch : 12 + 2 * branch, :]
        )
        grad = hidden_grad * silu_slope(value)
        normed_grads[branch][...] = grad
        sums[2 * branch : 2 * branch + 1, :] = column_sum(grad)
        sums[2 * branch + 1 : 2 * branch + 2, :] = column_sum(grad * scaled)
        write_edges(first, last, grad, branch, count, 0)


def finish_grads(packed, meta, stage, unite_grads, outs, scratch):
    if packed:
        pack_grads(meta[2], stage, unite_grads, outs, scratch)
    else:
        for ref, value in zip(outs, stage):
            ref[...] = value[...]


def kernel_grad_second(rows, counts, packed, meta, *refs):
    ins, unite_grads, outs, stage, scratch, hidden, sides, products = split_refs(
        refs, 16, 3, 4, 5, 3, 4, 4, 4
    )
    grads, seconds, firsts = ins[0:4], ins[4:8], ins[8:12]
    stat, stat_sums, first_stat, norms = ins[12:16]
    for branch in range(4):
        count, channels, total = rows[branch], CHANNELS[branch], counts[branch]
        stats = moments(stat[2 * branch : 2 * branch + 2, :], channels, total)
        grad = norm_input_grad(
            grads[branch][...],
            (seconds[branch][...] - stats[0]) * stats[1],
            stats,
            norms[2 * branch + 1 : 2 * branch + 2, :],
            stat_sums[2 * branch : 2 * branch + 2, :],
            channels,
            total,
        )
        fill_hidden(meta, firsts, first_stat, norms, hidden, branch, count, total)
        build_sides(hidden[branch], sides[branch], channels)
        products[branch][...] = dot_tn(patches(hidden[branch], sides[branch], count), grad)
        collect_band(products[branch], branch, tap_writer(stage[3 - branch], branch))
    finish_grads(packed, meta, stage, unite_grads, outs, scratch)


def kernel_grad_first(rows, counts, packed, meta, *refs):
    ins, unite_grads, outs, stage, scratch, sources, sides, products = split_refs(
        refs, 15, 3, 4, 5, 3, 4, 4, 4
    )
    grads, firsts, tiles = ins[0:4], ins[4:8], ins[8:12]
    first_stat, first_sums, norms = ins[12:15]
    for branch in range(4):
        count, channels, total = rows[branch], CHANNELS[branch], counts[branch]
        stats = moments(first_stat[2 * branch : 2 * branch + 2, :], channels, total)
        grad = norm_input_grad(
            grads[branch][...],
            (load_rows(firsts[branch], 1, count) - stats[0]) * stats[1],
            stats,
            norms[2 * branch : 2 * branch + 1, :],
            first_sums[2 * branch : 2 * branch + 2, :],
            channels,
            total,
        )
        sources[branch][...] = tiles[branch][:, 16 : (count + 3) * 16, :]
        build_sides(sources[branch], sides[branch], channels)
        products[branch][...] = dot_tn(patches(sources[branch], sides[branch], count), grad)
        collect_band(products[branch], branch, tap_writer(stage[3 - branch], branch))
    finish_grads(packed, meta, stage, unite_grads, outs, scratch)


def back_first_kernel(rows, counts, flags, *refs):
    ins, source_grads, wide, sides, bands = split_refs(refs, 21, 4, 4, 4, 4)
    normed_grads, firsts, join_grads, taps = ins[0:4], ins[4:8], ins[8:12], ins[12:16]
    above, below, first_stat, first_sums, norms = ins[16:21]
    for branch in range(4):
        count, channels, total = rows[branch], CHANNELS[branch], counts[branch]
        stats = moments(first_stat[2 * branch : 2 * branch + 2, :], channels, total)
        gain = norms[2 * branch : 2 * branch + 1, :]
        shift_sum = fold(first_sums[2 * branch : 2 * branch + 1, :], channels) / total
        gain_sum = fold(first_sums[2 * branch + 1 : 2 * branch + 2, :], channels) / total

        def input_grad(grad, value):
            scaled = (value - stats[0]) * stats[1]
            return (gain * stats[1]) * (grad - shift_sum - scaled * gain_sum)

        inner = input_grad(normed_grads[branch][...], load_rows(firsts[branch], 1, count))
        wide[branch][:, 16 : (count + 1) * 16, :] = inner.reshape(2, count * 16, 256)
        for image in range(2):
            place = edge_place(branch, image)
            for ref, start, flag in ((above, 0, flags[0]), (below, (count + 1) * 16, flags[1])):
                value = input_grad(
                    ref[place : place + 16, :], firsts[branch][image, start : start + 16, :]
                )
                wide[branch][image, start : start + 16, :] = jnp.where(flag == 0, 0.0, value)
        build_sides(wide[branch], sides[branch], channels)
        build_band(bands[branch], turned(tap_reader(taps[3 - branch], branch)), branch, 0)
        grad = dot_nn(patches(wide[branch], sides[branch], count), bands[branch][...])
        grad = (grad + join_grads[branch][...]).reshape(2, count * 16, 256)
        for image in range(2):
            source_grads[branch][image] = grad[image].reshape(count, 4096)


def finish_kernel(first_sums, second_sums, head_sums, gain, shift, loss, head_weight, head_bias):
    offset = 0

    def put(sums, line, channels):
        nonlocal offset
        for ref, row in ((shift, line), (gain, line + 1)):
            ref[0:1, offset : offset + channels] = fold(sums[row : row + 1, :], channels)[:, :channels]
        offset += channels

    for branch in range(4):
        for sums in (first_sums, second_sums):
            put(sums, 2 * branch, CHANNELS[branch])
    for level in range(3):
        put(head_sums, 2 * level, C0)
    loss[...] = jnp.sum(head_sums[6:7, :], axis=1, keepdims=True)
    joints = head_bias.shape[1]
    head_bias[...] = fold(head_sums[7:8, :], C0)[:, :joints]
    for part in range(4):
        head_weight[8 * part : 8 * part + 8, :] = head_sums[16:24, C0 * part : C0 * part + joints]


def device_count():
    return lax.axis_size("dp") * lax.axis_size("space")


def exchange(value, bit):
    return lax.ppermute(value, AXES, [(i, i ^ bit) for i in range(device_count())])


def total_sum(value, order=None):
    value = value.value
    for bit in order or [1 << i for i in range(device_count().bit_length() - 1)]:
        value = value + exchange(value, bit)
    return Kept(value)


def move_rows(first, last):
    devices = lax.axis_size("space")
    down = [(i, i + 1) for i in range(devices - 1)]
    up = [(i + 1, i) for i in range(devices - 1)]
    return lax.ppermute(last, "space", down), lax.ppermute(first, "space", up)


def device_index():
    return lax.axis_index("dp") * lax.axis_size("space") + lax.axis_index("space")


def gather_halves(shard):
    first_half = (device_index() & 16) == 0
    other = exchange(shard, 16)
    halves = []
    for own in (jnp.where(first_half, shard, other), jnp.where(first_half, other, shard)):
        far = exchange(own, 8)
        packs = []
        for cut, order in zip((slice(0, SPLIT), slice(SPLIT, SHARD)), GATHER_ORDER):
            part = jnp.stack([own[cut], far[cut]])
            for bit in order[1::-1]:
                part = jnp.concatenate([part, exchange(part, bit)])
            packs += [part, exchange(part, 1)]
        halves.append(packs)
    return halves


def scatter_half(packs):
    parts = []
    for keep, send, order in zip(packs[0::2], packs[1::2], SCATTER_ORDER):
        value = keep + exchange(send, 1)
        for bit in order:
            half = value.shape[0] // 2
            value = value[:half] + exchange(value[half:], bit)
        parts.append(value[0])
    return jnp.concatenate(parts)


def body(
    branch_zero,
    branch_one,
    branch_two,
    branch_three,
    convs_zero,
    convs_one,
    convs_two,
    convs_three,
    unite_one,
    unite_two,
    unite_three,
    norm_gain,
    norm_shift,
    head_weight,
    head_bias,
    targets,
    crowd_mask,
    person_count,
    flip_order,
):
    inputs = (branch_zero, branch_one, branch_two, branch_three)
    devices = device_count()
    spaces = lax.axis_size("space")
    place = lax.axis_index("space")
    rows = tuple(value.shape[1] for value in inputs)
    counts = tuple(
        float(2 * rows[b] * 16 * (256 // CHANNELS[b]) * devices) for b in range(4)
    )
    joints = head_bias.shape[0]
    cells = [2 * rows[b] * 16 for b in range(4)]
    packed = devices == 32
    shards_in = (convs_three, convs_two, convs_one, convs_zero, unite_one, unite_two, unite_three)
    sizes = [part.shape[0] for part in shards_in]

    if packed:
        gap = jnp.zeros(((24 - ROWS_ONE) * 128,), f32)
        flat = jnp.concatenate([*shards_in[:3], gap, *shards_in[3:]])
        first_packs, second_packs = gather_halves(flat.reshape(SHARD, 128))
    else:
        whole = [lax.all_gather(part, AXES, axis=0, tiled=True) for part in shards_in]
        whole = [
            part.reshape(-1, width)
            for part, width in zip(whole, (128, 128, 64, 32, 32, 32, 32))
        ]
        first_packs = [part[: part.shape[0] // 2] for part in whole]
        second_packs = [part[part.shape[0] // 2 :] for part in whole]

    last_rows = jnp.concatenate([value[:, -2:] for value in inputs], axis=1)
    first_rows = jnp.concatenate([value[:, :2] for value in inputs], axis=1)
    tops, bottoms = move_rows(first_rows, last_rows)
    meta = jnp.stack([place > 0, place < spaces - 1, device_index() & 15]).astype(jnp.int32)

    (norms,) = call(norm_kernel, [norm_gain[None], norm_shift[None]], kept([(22, 256)]), limit=4)

    def head_parts(weight, bias):
        weight = jnp.pad(weight, ((0, 0), (0, C0 - joints)))
        bias = jnp.tile(jnp.pad(bias, (0, C0 - joints)), 8)[None]
        return weight, bias

    weight, bias = head_parts(head_weight, head_bias)
    flip_weight, flip_bias = head_parts(head_weight[:, flip_order], head_bias[flip_order])
    target_cells = jnp.pad(
        jnp.transpose(targets.reshape(2, joints, rows[0], 16, 8), (0, 2, 3, 4, 1)),
        ((0, 0),) * 4 + ((0, C0 - joints),),
    ).reshape(cells[0], 256)
    loss_weight = crowd_mask.astype(f32) / person_count.astype(f32)[:, None, None]
    loss_weight = jnp.broadcast_to(
        loss_weight.reshape(2, rows[0], 16, 8, 1), (2, rows[0], 16, 8, C0)
    ).reshape(cells[0], 256)
    first_meta, weight, bias, flip_weight, flip_bias, target_cells, loss_weight = (
        lax.optimization_barrier(
            (meta, weight, bias, flip_weight, flip_bias, target_cells, loss_weight)
        )
    )

    bands = [band_shape(b, 256) for b in range(4)]
    inner = [(cells[b], 256) for b in range(4)]
    wide = [(2, (rows[b] + 2) * 16, 256) for b in range(4)]
    wider = [(2, (rows[b] + 4) * 16, 256) for b in range(4)]

    def sides_of(shapes):
        return [shape[:2] + (SIDES[b],) for b, shape in enumerate(shapes)]

    eight = (8, 256)
    taps_out = kept(TAPS_OUT) if packed else []
    unpack_scratch = list(PACK_SCRATCH) if packed else []

    out = call(
        functools.partial(first_kernel, rows, packed),
        [first_meta, *inputs, tops, bottoms, *first_packs[:4]],
        kept([*wider, *wide, eight]) + taps_out,
        bands + sides_of(wider) + unpack_scratch,
        smem=1,
        cost=7,
    )
    tiles, firsts = out[0:4], out[4:8]
    first_taps = out[9:] if packed else first_packs
    first_stat = total_sum(out[8])

    out = call(
        functools.partial(second_kernel, rows, counts, packed),
        [meta, *firsts, first_stat, norms, *second_packs[:4]],
        kept([*inner, eight]) + taps_out,
        wide + bands + sides_of(wide) + unpack_scratch,
        smem=1,
        cost=7,
    )
    seconds = out[0:4]
    second_taps = out[5:] if packed else second_packs
    unites = [*first_taps[4:7], *second_taps[4:7]]
    first_taps, second_taps = first_taps[:4], second_taps[:4]
    second_stat = total_sum(out[4])

    out = call(
        functools.partial(third_kernel, rows, counts),
        [*seconds[1:], *tiles[1:], second_stat, norms, *unites],
        kept([*inner[1:], eight]),
    )
    mixes = out[0:3]
    mix_stat = total_sum(out[3])

    denominator = float(counts[0] * joints)
    out = call(
        functools.partial(loss_kernel, rows, counts, denominator),
        [
            seconds[0],
            tiles[0],
            second_stat,
            *mixes,
            mix_stat,
            norms,
            weight,
            bias,
            target_cells,
            loss_weight,
        ],
        kept([inner[0], *inner[1:], (24, 256), inner[0]]),
        cost=3,
    )
    heat, pre_sums, join_zero = out[0], out[1:4], out[5]
    head_sums = total_sum(out[4])

    unite_shapes = [(CHANNELS[b], C0) for b in range(1, 4)]
    out = call(
        functools.partial(join_kernel, rows, counts),
        [
            *pre_sums,
            *mixes,
            *seconds,
            *tiles[1:],
            join_zero,
            second_stat,
            mix_stat,
            head_sums,
            norms,
            *unites,
        ],
        kept([*inner[1:], *unite_shapes, eight]) + [(256, 256), (256, 256)],
        cost=2,
    )
    join_grads = [join_zero, *out[0:3]]
    mixer_grads = [part.value for part in out[3:6]]
    first_mixers = [part[: part.shape[0] // 2] for part in mixer_grads]
    second_mixers = [part[part.shape[0] // 2 :] for part in mixer_grads]
    above, below = move_rows(out[7], out[8])
    second_sums = total_sum(out[6]).value
    second_sums = Kept(jnp.concatenate([head_sums.value[8:10], second_sums[2:8]]))

    out = call(
        functools.partial(back_second_kernel, rows, counts),
        [
            meta,
            *join_grads,
            *seconds,
            *firsts,
            *second_taps,
            above,
            below,
            second_stat,
            second_sums,
            first_stat,
            norms,
        ],
        kept([*inner, eight]) + [(128, 256), (128, 256)],
        wide + sides_of(wide) + bands,
        smem=1,
        cost=7,
    )
    normed_grads = out[0:4]
    above, below = move_rows(out[5], out[6])
    first_sums = total_sum(out[4])

    grads_out = list(PACKS) if packed else list(TAPS_OUT[:4])
    second_kernels = call(
        functools.partial(kernel_grad_second, rows, counts, packed),
        [
            meta,
            *join_grads,
            *seconds,
            *firsts,
            second_stat,
            second_sums,
            first_stat,
            norms,
            *second_mixers,
        ],
        grads_out,
        [*STAGE, *PACK_SCRATCH] + wide + sides_of(wide) + bands,
        smem=1,
        cost=8,
    )
    first_kernels = call(
        functools.partial(kernel_grad_first, rows, counts, packed),
        [
            meta,
            *normed_grads,
            *firsts,
            *tiles,
            first_stat,
            first_sums,
            norms,
            *first_mixers,
        ],
        grads_out,
        [*STAGE, *PACK_SCRATCH] + wide + sides_of(wide) + bands,
        smem=1,
        cost=7,
    )
    if packed:
        second_part = scatter_half(second_kernels)
        first_part = scatter_half(first_kernels)

    source_grads = call(
        functools.partial(back_first_kernel, rows, counts),
        [
            meta,
            *normed_grads,
            *firsts,
            *join_grads,
            *first_taps,
            above,
            below,
            first_stat,
            first_sums,
            norms,
        ],
        [value.shape for value in inputs],
        wide + sides_of(wide) + bands,
        smem=1,
        cost=7,
    )

    late_meta, _ = lax.optimization_barrier((meta, first_sums.value))
    flip_firsts = call(
        functools.partial(first_flip_kernel, rows),
        [late_meta, *tiles, *first_taps],
        kept(wide),
        bands + sides_of(wider),
        smem=1,
        cost=6,
    )
    flip_seconds = call(
        functools.partial(second_flip_kernel, rows, counts),
        [late_meta, *flip_firsts, first_stat, norms, *second_taps],
        kept(inner),
        wide + bands + sides_of(wide),
        smem=1,
        cost=6,
    )
    (heat_mean,) = call(
        functools.partial(flip_kernel, rows, counts),
        [
            *flip_seconds,
            *tiles,
            second_stat,
            *unites,
            mix_stat,
            norms,
            flip_weight,
            flip_bias,
            heat,
        ],
        [inner[0]],
        cost=2,
    )

    if packed:
        first_half = (device_index() & 16) == 0
        shard = jnp.where(first_half, first_part, second_part)
        shard = shard + exchange(jnp.where(first_half, second_part, first_part), 16)
        top = ROWS_THREE + ROWS_TWO + ROWS_ONE
        shard = jnp.concatenate([shard[:top].reshape(-1), shard[-8:].reshape(-1)])
        shards, offset = [], 0
        for size in sizes:
            shards.append(shard[offset : offset + size])
            offset += size
    else:
        flat = [
            jnp.concatenate([one.reshape(-1), two.reshape(-1)])
            for one, two in zip([*first_kernels, *first_mixers], [*second_kernels, *second_mixers])
        ]
        shards = [lax.psum_scatter(part, AXES, scatter_dimension=0, tiled=True) for part in flat]

    gain_grad, shift_grad, loss, head_grad, bias_grad = call(
        finish_kernel,
        [first_sums, second_sums, head_sums],
        [norm_gain[None].shape, norm_shift[None].shape, (1, 1), head_weight.shape, (1, joints)],
        limit=4,
    )
    heat_mean = jnp.transpose(
        heat_mean.reshape(2, rows[0], 16, 8, C0)[..., :joints], (0, 4, 1, 2, 3)
    ).reshape(targets.shape)
    return (
        loss[0, 0],
        heat_mean,
        *source_grads,
        shards[3],
        shards[2],
        shards[1],
        shards[0],
        *shards[4:7],
        gain_grad[0],
        shift_grad[0],
        head_grad,
        bias_grad[0],
    )


def solution(mesh):
    rows = P("dp", "space", None)
    shard = P(("dp", "space"))
    heat = P("dp", None, "space", None)
    return jax.shard_map(
        body,
        mesh=mesh,
        in_specs=(*[rows] * 4, *[shard] * 7, *[P()] * 4, heat, rows, P("dp"), P()),
        out_specs=(P(), heat, *[rows] * 4, *[shard] * 7, *[P()] * 4),
        check_vma=False,
    )
```

profile of v0, /device:TPU:0, one launch (start us, length us, event | category | flops | bytes accessed | tf_op | source)
XLA Modules:
  0.0 346.5 jit_solution(7986511760033883828)
XLA Ops:
  1.7 4.0 %collective-permute-start.2 = (f32[392,128]{1,0:T(8,128)S(1)}, f32[392,128]{1,0:T(8,128)S(1)}, u32[]{:S(2)}, u32[]{:S(2)}) collective-permute-start(f32[392,128]{1,0:T(8,128)S(1)} %bitcast.61), channel_id=1, source_target_pairs={{0,16},{1,17},{2,18},{3,19},{4,20},{5,21},{6,22},{7,23},{8,24},{9,... | collective-permute-start | bytes 602120 | tf_op jit(solution)/shard_map/ppermute | solution.py:785
  21.7 4.2 %reshape.68.refs_11_ = f32[1024,256]{1,0:T(8,128)} reshape(f32[2,32,16,8,32]{4,3,2,1,0:T(8,128)} %broadcast_in_dim.23) | data formatting | bytes 2097152 | tf_op jit(solution)/shard_map/reshape | solution.py:902
  28.6 4.8 %pad.22.clone = f32[2,32,16,8,32]{4,3,2,1,0:T(8,128)} pad(f32[2,32,16,8,17]{4,3,2,1,0:T(8,128)} %bitcast.60, f32[]{:T(128)} %constant.22.clone.1), padding=0_0x0_0x0_0x0_0x0_15 | pad | bytes 1605636 | tf_op jit(solution)/shard_map/jit(_pad)/pad | solution.py:895
  33.4 4.2 %reshape.67.refs_10_ = f32[1024,256]{1,0:T(8,128)} reshape(f32[2,32,16,8,32]{4,3,2,1,0:T(8,128)} %pad.22.clone) | data formatting | bytes 2097152 | tf_op jit(solution)/shard_map/reshape | solution.py:898
  39.9 8.9 %collective-permute-done.3 = f32[392,128]{1,0:T(8,128)S(1)} collective-permute-done((f32[392,128]{1,0:T(8,128)S(1)}, f32[392,128]{1,0:T(8,128)S(1)}, u32[]{:S(2)}, u32[]{:S(2)}) %collective-permute-start.3) | collective-permute-done | bytes 200736 | tf_op jit(solution)/shard_map/ppermute | solution.py:785
  52.6 4.0 %collective-permute-done.7 = f32[2,192,128]{2,1,0:T(8,128)S(1)} collective-permute-done((f32[2,192,128]{2,1,0:T(8,128)S(1)}, f32[2,192,128]{2,1,0:T(8,128)S(1)}, u32[]{:S(2)}, u32[]{:S(2)}) %collective-permute-start.7) | collective-permute-done | bytes 196640 | tf_op jit(solution)/shard_map/ppermute | solution.py:785
  62.5 6.3 %collective-permute-done.8 = f32[4,192,128]{2,1,0:T(8,128)S(1)} collective-permute-done((f32[4,192,128]{2,1,0:T(8,128)S(1)}, f32[4,192,128]{2,1,0:T(8,128)S(1)}, u32[]{:S(2)}, u32[]{:S(2)}) %collective-permute-start.8) | collective-permute-done | bytes 393248 | tf_op jit(solution)/shard_map/ppermute | solution.py:785
  74.4 6.2 %collective-permute-done.20 = f32[4,192,128]{2,1,0:T(8,128)S(1)} collective-permute-done((f32[4,192,128]{2,1,0:T(8,128)S(1)}, f32[4,192,128]{2,1,0:T(8,128)S(1)}, u32[]{:S(2)}, u32[]{:S(2)}) %collective-permute-start.20) | collective-permute-done | bytes 393248 | tf_op jit(solution)/shard_map/ppermute | solution.py:785
  86.0 8.8 %shard_map.314 = (f32[2,576,256]{2,1,0:T(8,128)S(1)}, f32[2,320,256]{2,1,0:T(8,128)S(1)}, f32[2,192,256]{2,1,0:T(8,128)S(1)}, f32[2,128,256]{2,1,0:T(8,128)S(1)}...) custom-call(s32[3]{0:T(128)S(1)} %pad_add_fusion.meta.flags, ...), custom_call_target="tpu_custom_call" | custom-call | flops 7699999744 | bytes 21000000 | tf_op jit(solution)/shard_map/pallas_call | solution.py:328
  116.0 8.5 %shard_map.316 = (f32[1024,256]{1,0:T(8,128)S(1)}, f32[512,256]{1,0:T(8,128)S(1)}, f32[256,256]{1,0:T(8,128)S(1)}, f32[128,256]{1,0:T(8,128)S(1)}, f32[8,256]{1,...) custom-call(s32[3]{0:T(128)S(1)} %pad_add_fusion.meta.flags, ...), custom_call_target="tpu_custom_call" | custom-call | flops 7699999744 | bytes 21000000 | tf_op jit(solution)/shard_map/pallas_call | solution.py:328
  137.2 4.1 %collective-permute-done.26 = f32[8,256]{1,0:T(8,128)S(1)} collective-permute-done((f32[8,256]{1,0:T(8,128)S(1)}, f32[8,256]{1,0:T(8,128)S(1)}, u32[]{:S(2)}, u32[]{:S(2)}) %collective-permute-start.26) | collective-permute-done | bytes 8224 | tf_op jit(solution)/shard_map/ppermute | solution.py:785
  154.8 4.0 %collective-permute-done.31 = f32[8,256]{1,0:T(8,128)S(1)} collective-permute-done((f32[8,256]{1,0:T(8,128)S(1)}, f32[8,256]{1,0:T(8,128)S(1)}, u32[]{:S(2)}, u32[]{:S(2)}) %collective-permute-start.31) | collective-permute-done | bytes 8224 | tf_op jit(solution)/shard_map/ppermute | solution.py:785
  158.9 4.3 %shard_map.318 = (f32[1024,256]{1,0:T(8,128)S(1)}, f32[512,256]{1,0:T(8,128)S(1)}, f32[256,256]{1,0:T(8,128)S(1)}, f32[128,256]{1,0:T(8,128)S(1)}, f32[24,256]{1,0:T(8,128)S(1)}, /*index=5*/f32[1024,256]{1,0:T(8,128)S(1)}) custom-call(f32[1024,256]{1,0:T(8,128)S(1)} %get-tuple-element.110.refs_0_.refs_6_.refs_4_, ...), custom_call_target="tpu_custom_call" | custom-call | flops 3300000000 | bytes 9000000 | tf_op jit(solution)/shard_map/pallas_call | solution.py:328
  176.4 4.2 %collective-permute-done.36 = f32[24,256]{1,0:T(8,128)S(1)} collective-permute-done((f32[24,256]{1,0:T(8,128)S(1)}, f32[24,256]{1,0:T(8,128)S(1)}, u32[]{:S(2)}, u32[]{:S(2)}) %collective-permute-start.36) | collective-permute-done | bytes 24608 | tf_op jit(solution)/shard_map/ppermute | solution.py:785
  201.8 7.2 %shard_map.320 = (f32[1024,256]{1,0:T(8,128)S(1)}, f32[512,256]{1,0:T(8,128)S(1)}, f32[256,256]{1,0:T(8,128)S(1)}, f32[128,256]{1,0:T(8,128)S(1)}, f32[8,256]{1,...) custom-call(s32[3]{0:T(128)S(1)} %pad_add_fusion.meta.flags, ...), custom_call_target="tpu_custom_call" | custom-call | flops 7699999744 | bytes 21000000 | tf_op jit(solution)/shard_map/pallas_call | solution.py:328
  209.0 4.8 %collective-permute-start.44 = (f32[8,256]{1,0:T(8,128)S(1)}, f32[8,256]{1,0:T(8,128)S(1)}, u32[]{:S(2)}, u32[]{:S(2)}) collective-permute-start(f32[8,256]{1,0:T(8,128)S(1)} %get-tuple-element.148), channel_id=1, source_target_pairs={{0,1},{1,0},{2,3},{3,2},{4,5},{5,4},{6,7},{7,6},{8,9},{9,8},{10,11... | collective-permute-start | bytes 24584 | tf_op jit(solution)/shard_map/ppermute | solution.py:785
  228.0 9.1 %shard_map.327 = (f32[8,200,128]{2,1,0:T(8,128)}, f32[8,200,128]{2,1,0:T(8,128)}, f32[8,192,128]{2,1,0:T(8,128)}, f32[8,192,128]{2,1,0:T(8,128)}) custom-call(s32[3]{0:T(128)S(1)} %pad_add_fusion.meta.flags, f32[1024,256]{1,0:T(8,128)S(1)} %get-tuple-element.133.refs_13_.refs_0_.refs_8_, f32[512,256]{1,0:T(8,128)S(1)} %get-tuple-element.138.refs_1_.refs_9_, ...), custom_call_target="tpu_custom_call" | custom-call | flops 8800000000 | bytes 24000000 | tf_op jit(solution)/shard_map/pallas_call | solution.py:328
  240.2 8.1 %shard_map.326 = (f32[8,200,128]{2,1,0:T(8,128)}, f32[8,200,128]{2,1,0:T(8,128)}, f32[8,192,128]{2,1,0:T(8,128)}, f32[8,192,128]{2,1,0:T(8,128)}) custom-call(s32[3]{0:T(128)S(1)} %pad_add_fusion.meta.flags, f32[1024,256]{1,0:T(8,128)S(1)} %get-tuple-element.166.refs_0_, f32[512,256]{1,0:T(8,128)S(1)} %get-tuple-element.167.refs_1_, ...), custom_call_target="tpu_custom_call" | custom-call | flops 7699999744 | bytes 21000000 | tf_op jit(solution)/shard_map/pallas_call | solution.py:328
  248.8 5.9 %shard_map.322 = (f32[2,544,256]{2,1,0:T(8,128)S(1)}, f32[2,288,256]{2,1,0:T(8,128)S(1)}, f32[2,160,256]{2,1,0:T(8,128)S(1)}, f32[2,96,256]{2,1,0:T(8,128)S(1)}) custom-call(s32[3]{0:T(128)S(1)} %pad_add_fusion.meta.flags, f32[2,576,256]{2,1,0:T(8,128)S(1)} %get-tuple-element.111.refs_1_.refs_0_.refs_4_.refs_8_, ...), custom_call_target="tpu_custom_call" | custom-call | flops 6600000000 | bytes 18000000 | tf_op jit(solution)/shard_map/pallas_call | solution.py:328
  254.7 6.5 %shard_map.323 = (f32[1024,256]{1,0:T(8,128)S(1)}, f32[512,256]{1,0:T(8,128)S(1)}, f32[256,256]{1,0:T(8,128)S(1)}, f32[128,256]{1,0:T(8,128)S(1)}) custom-call(s32[3]{0:T(128)S(1)} %pad_add_fusion.meta.flags, f32[2,544,256]{2,1,0:T(8,128)S(1)} %get-tuple-element.155.refs_0_, f32[2,288,256]{2,1,0:T(8,128)S(1)} %get-tuple-element.156.refs_1_, ...), custom_call_target="tpu_custom_call" | custom-call | flops 6600000000 | bytes 18000000 | tf_op jit(solution)/shard_map/pallas_call | solution.py:328
  298.2 11.4 %collective-permute-done.65 = f32[2,192,128]{2,1,0:T(8,128)S(1)} collective-permute-done((f32[2,192,128]{2,1,0:T(8,128)S(1)}, f32[2,192,128]{2,1,0:T(8,128)S(1)}, u32[]{:S(2)}, u32[]{:S(2)}) %collective-permute-start.65) | collective-permute-done | bytes 196640 | tf_op jit(solution)/shard_map/ppermute | solution.py:785
  310.0 6.0 %collective-permute-done.61 = f32[2,200,128]{2,1,0:T(8,128)S(1)} collective-permute-done((f32[2,200,128]{2,1,0:T(8,128)S(1)}, f32[2,200,128]{2,1,0:T(8,128)S(1)}, u32[]{:S(2)}, u32[]{:S(2)}) %collective-permute-start.61) | collective-permute-done | bytes 204832 | tf_op jit(solution)/shard_map/ppermute | solution.py:785
  322.3 4.0 %collective-permute-done.57 = f32[2,192,128]{2,1,0:T(8,128)S(1)} collective-permute-done((f32[2,192,128]{2,1,0:T(8,128)S(1)}, f32[2,192,128]{2,1,0:T(8,128)S(1)}, u32[]{:S(2)}, u32[]{:S(2)}) %collective-permute-start.57) | collective-permute-done | bytes 196640 | tf_op jit(solution)/shard_map/ppermute | solution.py:785
  335.0 7.4 %shard_map.325 = (f32[2,32,4096]{2,1,0:T(8,128)}, f32[2,16,4096]{2,1,0:T(8,128)}, f32[2,8,4096]{2,1,0:T(8,128)}, f32[2,4,4096]{2,1,0:T(4,128)}) custom-call(s32[3]{0:T(128)S(1)} %pad_add_fusion.meta.flags, f32[1024,256]{1,0:T(8,128)S(1)} %copy-done.3, f32[512,256]{1,0:T(8,128)S(1)} %copy-done.9, f32[256,256]{1,0:T(8,128)S(1)} %copy-done.13, ...), custom_call_target="tpu_custom_call" | custom-call | flops 7699999744 | bytes 21000000 | tf_op jit(solution)/shard_map/pallas_call | solution.py:328
  (341 shorter events, 198.0 us)
Async XLA Ops:
  1.7 35.9 %collective-permute-start.2 = (f32[392,128]{1,0:T(8,128)S(1)}, f32[392,128]{1,0:T(8,128)S(1)}, u32[]{:S(2)}, u32[]{:S(2)}) collective-permute-start(f32[392,128]{1,0:T(8,128)S(1)} %bitcast.61), channel_id=1, source_target_pairs={{0,16},{1,17},{2,18},{3,19},{4,20},{5,21},{6,22},{7,23},{8,24},{9,... | collective-permute-start | bytes 602120 | tf_op jit(solution)/shard_map/ppermute | solution.py:785
  8.3 75.3 %collective-permute-start = (f32[2,8,4096]{2,1,0:T(8,128)S(1)}, f32[2,8,4096]{2,1,0:T(8,128)S(1)}, u32[]{:S(2)}, u32[]{:S(2)}) collective-permute-start(f32[2,8,4096]{2,1,0:T(8,128)S(1)} %pad_maximum_fusion.8), channel_id=1, source_target_pairs={{0,1},{1,2},{2,3},{4,5},{5,6},{6,7},{8,9},{9,10},{10,11},{12,13},{... | collective-permute-start | bytes 786440 | tf_op jit(solution)/shard_map/ppermute | solution.py:799
  37.7 13.8 %collective-permute-start.15 = (f32[392,128]{1,0:T(8,128)S(1)}, f32[392,128]{1,0:T(8,128)S(1)}, u32[]{:S(2)}, u32[]{:S(2)}) collective-permute-start(f32[392,128]{1,0:T(8,128)S(1)} %get-tuple-element.246), channel_id=1, source_target_pairs={{0,8},{1,9},{2,10},{3,11},{4,12},{5,13},{6,14},{7,15},{8,0},{9,1},... | collective-permute-start | bytes 602120 | tf_op jit(solution)/shard_map/ppermute | solution.py:785
  56.7 12.0 %collective-permute-start.8 = (f32[4,192,128]{2,1,0:T(8,128)S(1)}, f32[4,192,128]{2,1,0:T(8,128)S(1)}, u32[]{:S(2)}, u32[]{:S(2)}) collective-permute-start(f32[4,192,128]{2,1,0:T(8,128)S(1)} %pad_maximum_fusion.6), channel_id=1, source_target_pairs={{0,4},{1,5},{2,6},{3,7},{4,0},{5,1},{6,2},{7,3},{8,12},{9,13},{10,... | collective-permute-start | bytes 1179656 | tf_op jit(solution)/shard_map/ppermute | solution.py:785
  58.3 11.3 %collective-permute-start.5 = (f32[4,200,128]{2,1,0:T(8,128)S(1)}, f32[4,200,128]{2,1,0:T(8,128)S(1)}, u32[]{:S(2)}, u32[]{:S(2)}) collective-permute-start(f32[4,200,128]{2,1,0:T(8,128)S(1)} %pad_maximum_fusion.4), channel_id=1, source_target_pairs={{0,2},{1,3},{2,0},{3,1},{4,6},{5,7},{6,4},{7,5},{8,10},{9,11},{10,... | collective-permute-start | bytes 1228808 | tf_op jit(solution)/shard_map/ppermute | solution.py:785
  59.4 13.7 %collective-permute-start.16 = (f32[2,200,128]{2,1,0:T(8,128)S(1)}, f32[2,200,128]{2,1,0:T(8,128)S(1)}, u32[]{:S(2)}, u32[]{:S(2)}) collective-permute-start(f32[2,200,128]{2,1,0:T(8,128)S(1)} %pad_maximum_fusion.11), channel_id=1, source_target_pairs={{0,4},{1,5},{2,6},{3,7},{4,0},{5,1},{6,2},{7,3},{8,12},{9,13},{10,... | collective-permute-start | bytes 614408 | tf_op jit(solution)/shard_map/ppermute | solution.py:785
  60.9 19.8 %collective-permute-start.20 = (f32[4,192,128]{2,1,0:T(8,128)S(1)}, f32[4,192,128]{2,1,0:T(8,128)S(1)}, u32[]{:S(2)}, u32[]{:S(2)}) collective-permute-start(f32[4,192,128]{2,1,0:T(8,128)S(1)} %pad_maximum_fusion.7), channel_id=1, source_target_pairs={{0,4},{1,5},{2,6},{3,7},{4,0},{5,1},{6,2},{7,3},{8,12},{9,13},{10,... | collective-permute-start | bytes 1179656 | tf_op jit(solution)/shard_map/ppermute | solution.py:785
  68.8 15.3 %collective-permute-start.9 = (f32[8,192,128]{2,1,0:T(8,128)S(1)}, f32[8,192,128]{2,1,0:T(8,128)S(1)}, u32[]{:S(2)}, u32[]{:S(2)}) collective-permute-start(f32[8,192,128]{2,1,0:T(8,128)S(1)} %pad_maximum_fusion.2.refs_8_), channel_id=1, source_target_pairs={{0,1},{1,0},{2,3},{3,2},{4,5},{5,4},{6,7},{7,6},{8,9},{9,8},{10,11... | collective-permute-start | bytes 2359304 | tf_op jit(solution)/shard_map/ppermute | solution.py:785
  69.7 14.4 %collective-permute-start.6 = (f32[8,200,128]{2,1,0:T(8,128)S(1)}, f32[8,200,128]{2,1,0:T(8,128)S(1)}, u32[]{:S(2)}, u32[]{:S(2)}) collective-permute-start(f32[8,200,128]{2,1,0:T(8,128)S(1)} %pad_maximum_fusion.refs_6_), channel_id=1, source_target_pairs={{0,1},{1,0},{2,3},{3,2},{4,5},{5,4},{6,7},{7,6},{8,9},{9,8},{10,11... | collective-permute-start | bytes 2457608 | tf_op jit(solution)/shard_map/ppermute | solution.py:785
  73.2 9.8 %collective-permute-start.17 = (f32[4,200,128]{2,1,0:T(8,128)S(1)}, f32[4,200,128]{2,1,0:T(8,128)S(1)}, u32[]{:S(2)}, u32[]{:S(2)}) collective-permute-start(f32[4,200,128]{2,1,0:T(8,128)S(1)} %pad_maximum_fusion.5), channel_id=1, source_target_pairs={{0,2},{1,3},{2,0},{3,1},{4,6},{5,7},{6,4},{7,5},{8,10},{9,11},{10,... | collective-permute-start | bytes 1228808 | tf_op jit(solution)/shard_map/ppermute | solution.py:785
  82.9 31.9 %collective-permute-start.21 = (f32[8,192,128]{2,1,0:T(8,128)S(1)}, f32[8,192,128]{2,1,0:T(8,128)S(1)}, u32[]{:S(2)}, u32[]{:S(2)}) collective-permute-start(f32[8,192,128]{2,1,0:T(8,128)S(1)} %pad_maximum_fusion.3.refs_8_), channel_id=1, source_target_pairs={{0,1},{1,0},{2,3},{3,2},{4,5},{5,4},{6,7},{7,6},{8,9},{9,8},{10,11... | collective-permute-start | bytes 2359304 | tf_op jit(solution)/shard_map/ppermute | solution.py:785
  83.6 31.2 %collective-permute-start.18 = (f32[8,200,128]{2,1,0:T(8,128)S(1)}, f32[8,200,128]{2,1,0:T(8,128)S(1)}, u32[]{:S(2)}, u32[]{:S(2)}) collective-permute-start(f32[8,200,128]{2,1,0:T(8,128)S(1)} %pad_maximum_fusion.1.refs_6_), channel_id=1, source_target_pairs={{0,1},{1,0},{2,3},{3,2},{4,5},{5,4},{6,7},{7,6},{8,9},{9,8},{10,11... | collective-permute-start | bytes 2457608 | tf_op jit(solution)/shard_map/ppermute | solution.py:785
  225.7 14.4 %collective-permute-start.48 = (f32[8,256]{1,0:T(8,128)S(1)}, f32[8,256]{1,0:T(8,128)S(1)}, u32[]{:S(2)}, u32[]{:S(2)}) collective-permute-start(f32[8,256]{1,0:T(8,128)S(1)} %add.190), channel_id=1, source_target_pairs={{0,16},{1,17},{2,18},{3,19},{4,20},{5,21},{6,22},{7,23},{8,24},{9,... | collective-permute-start | bytes 24584 | tf_op jit(solution)/shard_map/ppermute | solution.py:785
  237.0 31.6 %collective-permute-start.63 = (f32[8,192,128]{2,1,0:T(8,128)}, f32[8,192,128]{2,1,0:T(8,128)}, u32[]{:S(2)}, u32[]{:S(2)}) collective-permute-start(f32[8,192,128]{2,1,0:T(8,128)} %get-tuple-element.186), channel_id=1, source_target_pairs={{0,1},{1,0},{2,3},{3,2},{4,5},{5,4},{6,7},{7,6},{8,9},{9,8},{10,11... | collective-permute-start | bytes 2359304 | tf_op jit(solution)/shard_map/ppermute | solution.py:785
  237.0 34.0 %collective-permute-start.59 = (f32[8,200,128]{2,1,0:T(8,128)}, f32[8,200,128]{2,1,0:T(8,128)}, u32[]{:S(2)}, u32[]{:S(2)}) collective-permute-start(f32[8,200,128]{2,1,0:T(8,128)} %get-tuple-element.184), channel_id=1, source_target_pairs={{0,1},{1,0},{2,3},{3,2},{4,5},{5,4},{6,7},{7,6},{8,9},{9,8},{10,11... | collective-permute-start | bytes 2457608 | tf_op jit(solution)/shard_map/ppermute | solution.py:785
  237.5 96.7 %collective-permute-start.49 = (f32[128,256]{1,0:T(8,128)}, f32[128,256]{1,0:T(8,128)}, u32[]{:S(2)}, u32[]{:S(2)}) collective-permute-start(f32[128,256]{1,0:T(8,128)} %get-tuple-element.170), channel_id=1, source_target_pairs={{0,1},{1,2},{2,3},{4,5},{5,6},{6,7},{8,9},{9,10},{10,11},{12,13},{... | collective-permute-start | bytes 393224 | tf_op jit(solution)/shard_map/ppermute | solution.py:799
  248.3 38.4 %collective-permute-start.55 = (f32[8,192,128]{2,1,0:T(8,128)}, f32[8,192,128]{2,1,0:T(8,128)}, u32[]{:S(2)}, u32[]{:S(2)}) collective-permute-start(f32[8,192,128]{2,1,0:T(8,128)} %get-tuple-element.182), channel_id=1, source_target_pairs={{0,1},{1,0},{2,3},{3,2},{4,5},{5,4},{6,7},{7,6},{8,9},{9,8},{10,11... | collective-permute-start | bytes 2359304 | tf_op jit(solution)/shard_map/ppermute | solution.py:785
  248.3 41.5 %collective-permute-start.51 = (f32[8,200,128]{2,1,0:T(8,128)}, f32[8,200,128]{2,1,0:T(8,128)}, u32[]{:S(2)}, u32[]{:S(2)}) collective-permute-start(f32[8,200,128]{2,1,0:T(8,128)} %get-tuple-element.180), channel_id=1, source_target_pairs={{0,1},{1,0},{2,3},{3,2},{4,5},{5,4},{6,7},{7,6},{8,9},{9,8},{10,11... | collective-permute-start | bytes 2457608 | tf_op jit(solution)/shard_map/ppermute | solution.py:785
  271.0 22.8 %collective-permute-start.64 = (f32[4,192,128]{2,1,0:T(8,128)}, f32[4,192,128]{2,1,0:T(8,128)}, u32[]{:S(2)}, u32[]{:S(2)}) collective-permute-start(f32[4,192,128]{2,1,0:T(8,128)} %slice.289), channel_id=1, source_target_pairs={{0,2},{1,3},{2,0},{3,1},{4,6},{5,7},{6,4},{7,5},{8,10},{9,11},{10,... | collective-permute-start | bytes 1179656 | tf_op jit(solution)/shard_map/ppermute | solution.py:785
  274.4 21.1 %collective-permute-start.60 = (f32[4,200,128]{2,1,0:T(8,128)}, f32[4,200,128]{2,1,0:T(8,128)}, u32[]{:S(2)}, u32[]{:S(2)}) collective-permute-start(f32[4,200,128]{2,1,0:T(8,128)} %slice.283), channel_id=1, source_target_pairs={{0,4},{1,5},{2,6},{3,7},{4,0},{5,1},{6,2},{7,3},{8,12},{9,13},{10,... | collective-permute-start | bytes 1228808 | tf_op jit(solution)/shard_map/ppermute | solution.py:785
  286.6 47.6 %collective-permute-start.50 = (f32[128,256]{1,0:T(8,128)}, f32[128,256]{1,0:T(8,128)S(1)}, u32[]{:S(2)}, u32[]{:S(2)}) collective-permute-start(f32[128,256]{1,0:T(8,128)} %get-tuple-element.171), channel_id=1, source_target_pairs={{1,0},{2,1},{3,2},{5,4},{6,5},{7,6},{9,8},{10,9},{11,10},{13,12},{... | collective-permute-start | bytes 393224 | tf_op jit(solution)/shard_map/ppermute | solution.py:799
  289.7 27.8 %collective-permute-start.56 = (f32[4,192,128]{2,1,0:T(8,128)S(1)}, f32[4,192,128]{2,1,0:T(8,128)S(1)}, u32[]{:S(2)}, u32[]{:S(2)}) collective-permute-start(f32[4,192,128]{2,1,0:T(8,128)S(1)} %slice.277), channel_id=1, source_target_pairs={{0,2},{1,3},{2,0},{3,1},{4,6},{5,7},{6,4},{7,5},{8,10},{9,11},{10,... | collective-permute-start | bytes 1179656 | tf_op jit(solution)/shard_map/ppermute | solution.py:785
  293.7 27.4 %collective-permute-start.52 = (f32[4,200,128]{2,1,0:T(8,128)S(1)}, f32[4,200,128]{2,1,0:T(8,128)S(1)}, u32[]{:S(2)}, u32[]{:S(2)}) collective-permute-start(f32[4,200,128]{2,1,0:T(8,128)S(1)} %slice.271), channel_id=1, source_target_pairs={{0,4},{1,5},{2,6},{3,7},{4,0},{5,1},{6,2},{7,3},{8,12},{9,13},{10,... | collective-permute-start | bytes 1228808 | tf_op jit(solution)/shard_map/ppermute | solution.py:785
  295.4 14.2 %collective-permute-start.65 = (f32[2,192,128]{2,1,0:T(8,128)S(1)}, f32[2,192,128]{2,1,0:T(8,128)S(1)}, u32[]{:S(2)}, u32[]{:S(2)}) collective-permute-start(f32[2,192,128]{2,1,0:T(8,128)S(1)} %slice.291), channel_id=1, source_target_pairs={{0,4},{1,5},{2,6},{3,7},{4,0},{5,1},{6,2},{7,3},{8,12},{9,13},{10,... | collective-permute-start | bytes 589832 | tf_op jit(solution)/shard_map/ppermute | solution.py:785
  (86 other events, 1743.8 us)
where the time goes:
time: 352 us; the launch traced here: 347 us
  waiting for transfers between devices  130 us (37%)
  Pallas kernels  74.4 us (21%)
  starting transfers between devices  72.5 us (21%)
  local copies, waits for them, and re-layouts  54.1 us (15%)
  other arithmetic  14.1 us (4%)
    ppermute x62, waiting for transfers between devices, exchange(): lax.ppermute(value, AXES, [(i, i ^ bit) for i in range(device_count())])  128 us
    pallas_call x14, Pallas kernels, call(): pl.pallas_call(kernel, in_specs=specs, out_specs=[pl.BlockSpec(memory_spa...  74.4 us
    ppermute x62, starting transfers between devices, exchange(): lax.ppermute(value, AXES, [(i, i ^ bit) for i in range(device_count())])  62.6 us
    unnamed x87, local copies, waits for them, and re-layouts  11.4 us
    ppermute x6, starting transfers between devices, move_rows(): return (lax.ppermute(last, 'space', down), lax.ppermute(first, 'space', up))  9.96 us
  transfers between devices with their start and end apart: 68, of which 46 were waited for; matrix products, arithmetic and copies ran while one was open for 17% of the time, Pallas kernels for 15%

commit v1 on v0

--- a/solution.py
+++ b/solution.py
@@ -196,39 +196,44 @@
     return emit
 
 
-SPLIT = 200
 SHARD = 392
 ROWS_THREE, ROWS_TWO, ROWS_ONE = 288, 72, 18
 PER_ZERO, PER_UNITE = 18, (2, 4, 8)
-GATHER_ORDER = ((2, 4, 8), (4, 2, 8))
-SCATTER_ORDER = ((4, 2, 8), (2, 4, 8))
+CHUNKS = ((0, 128), (128, 256), (256, 392))
+STEPS = ((8, 4, 2), (4, 2, 8), (2, 8, 4))
 TAPS_OUT = ((4608, 128), (1152, 128), (576, 64), (288, 32), (32, 32), (64, 32), (128, 32))
 PACK_SCRATCH = ((16, 24, 128), (16, 8, 128), (288, 128))
 STAGE = ((4608, 128), (1152, 128), (576, 64), (288, 32), (512, 32))
 
 
-def partner(me, core, place, order):
-    bits = sum(bit for i, bit in enumerate(order) if place >> (2 - i) & 1)
-    return me ^ (bits + core)
+def partner(me, core, place, bits):
+    return me ^ (core + sum(bit for i, bit in enumerate(bits) if place >> i & 1))
+
+
+def shard_parts(device, three, two, one, zero):
+    start = device * ROWS_THREE
+    return (
+        ((0, 128, three.at[pl.ds(pl.multiple_of(start, 8), 128), :]),),
+        ((128, 256, three.at[pl.ds(pl.multiple_of(start + 128, 8), 128), :]),),
+        (
+            (256, 288, three.at[pl.ds(pl.multiple_of(start + 256, 8), 32), :]),
+            (288, 360, two.at[pl.ds(pl.multiple_of(device * ROWS_TWO, 8), ROWS_TWO), :]),
+            (360, 384, one.at[device]),
+            (384, 392, zero.at[device]),
+        ),
+    )
 
 
 def unpack_taps(me, packs, taps, scratch):
     three, two, one, zero = taps[:4]
     part_one, part_zero, flat_one = scratch
     for core in range(2):
-        upper, lower = packs[core], packs[2 + core]
         for place in range(8):
-            device = partner(me, core, place, GATHER_ORDER[0])
-            start = pl.multiple_of(device * ROWS_THREE, 8)
-            three[pl.ds(start, SPLIT), :] = upper[place]
-            device = partner(me, core, place, GATHER_ORDER[1])
-            rest = ROWS_THREE - SPLIT
-            start = pl.multiple_of(device * ROWS_THREE + SPLIT, 8)
-            three[pl.ds(start, rest), :] = lower[place, 0:rest]
-            start = pl.multiple_of(device * ROWS_TWO, 8)
-            two[pl.ds(start, ROWS_TWO), :] = lower[place, rest : rest + ROWS_TWO]
-            part_one[device] = lower[place, rest + ROWS_TWO : rest + ROWS_TWO + 24]
-            part_zero[device] = lower[place, rest + ROWS_TWO + 24 :]
+            for chunk in range(3):
+                device = partner(me, core, place, STEPS[chunk])
+                parts = shard_parts(device, three, two, part_one, part_zero)[chunk]
+                for first, last, ref in parts:
+                    ref[...] = packs[core][place, first:last]
     for device in range(16):
         flat_one[device * ROWS_ONE : (device + 1) * ROWS_ONE, :] = part_one[device, 0:ROWS_ONE]
     one[...] = flat_one[...].reshape(one.shape)
@@ -253,22 +258,80 @@
             first += height
     part_zero[...] = narrow[...].reshape(128, 128).reshape(16, 8, 128)
     for core in range(2):
-        upper, lower = packs[core], packs[2 + core]
         for place in range(8):
-            device = partner(me, core, place, SCATTER_ORDER[0])
-            start = pl.multiple_of(device * ROWS_THREE, 8)
-            upper[place] = three[pl.ds(start, SPLIT), :]
-            device = partner(me, core, place, SCATTER_ORDER[1])
-            rest = ROWS_THREE - SPLIT
-            start = pl.multiple_of(device * ROWS_THREE + SPLIT, 8)
-            lower[place, 0:rest] = three[pl.ds(start, rest), :]
-            start = pl.multiple_of(device * ROWS_TWO, 8)
-            lower[place, rest : rest + ROWS_TWO] = two[pl.ds(start, ROWS_TWO), :]
-            lower[place, rest + ROWS_TWO : rest + ROWS_TWO + 24] = part_one[device]
-            lower[place, rest + ROWS_TWO + 24 :] = part_zero[device]
-
-
-PACKS = ((8, SPLIT, 128), (8, SPLIT, 128), (8, SHARD - SPLIT, 128), (8, SHARD - SPLIT, 128))
+            for chunk in range(3):
+                device = partner(me, core, place, STEPS[chunk][::-1])
+                parts = shard_parts(device, three, two, part_one, part_zero)[chunk]
+                for first, last, ref in parts:
+                    packs[core][place, first:last] = ref[...]
+
+
+def split_shard(meta, shard, other, *outs):
+    second = meta[3] == 1
+    for out, (first, last) in zip(outs, CHUNKS):
+        own, far = shard[first:last], other[first:last]
+        out[0, 0] = jnp.where(second, far, own)
+        out[0, 1] = jnp.where(second, own, far)
+
+
+def join_chunks(*refs):
+    held, received, outs = split_refs(refs, 3, 3, 3)
+    for chunk in range(3):
+        count = held[chunk].shape[0]
+        outs[chunk][0:count] = held[chunk][...]
+        outs[chunk][count : 2 * count] = received[chunk][...]
+
+
+def join_apart(*refs):
+    held, received, first, second = split_refs(refs, 3, 3, 3, 3)
+    for chunk in range(3):
+        count = held[chunk].shape[0]
+        for half, outs in ((0, first), (1, second)):
+            outs[chunk][0:count] = held[chunk][:, half]
+            outs[chunk][count : 2 * count] = received[chunk][:, half]
+
+
+def join_whole(*refs):
+    held, received, out = split_refs(refs, 3, 3, 1)
+    for chunk, (first, last) in enumerate(CHUNKS):
+        count = held[chunk].shape[0]
+        out[0][0:count, first:last] = held[chunk][...]
+        out[0][count : 2 * count, first:last] = received[chunk][...]
+
+
+def add_cores(*refs):
+    kept_ones, received, low, high = split_refs(refs, 2, 2, 3, 3)
+    for chunk, (first, last) in enumerate(CHUNKS):
+        for half in range(2):
+            total = kept_ones[half][:, first:last] + received[half][:, first:last]
+            low[chunk][:, half] = total[:4]
+            high[chunk][:, half] = total[4:]
+
+
+def add_received(*refs):
+    held, received, low, high = split_refs(refs, 3, 3, 3, 3)
+    for chunk in range(3):
+        half = held[chunk].shape[0] // 2
+        low[chunk][...] = held[chunk][0:half] + received[chunk][0:half]
+        high[chunk][...] = held[chunk][half:] + received[chunk][half:]
+
+
+def add_last(meta, *refs):
+    held, received, keep, send = split_refs(refs, 3, 3, 1, 1)
+    second = meta[3] == 1
+    for chunk, (first, last) in enumerate(CHUNKS):
+        total = held[chunk][0] + received[chunk][0]
+        keep[0][first:last, :] = jnp.where(second, total[1], total[0])
+        send[0][first:last, :] = jnp.where(second, total[0], total[1])
+
+
+def add_shard(keep, received, three, two, one, rest):
+    first = 0
+    for ref in (three, two, one):
+        last = first + ref.shape[0]
+        ref[...] = keep[first:last] + received[first:last]
+        first = last
+    rest[...] = keep[SHARD - 8 :] + received[SHARD - 8 :]
 
 
 def mirrored(tap):
@@ -343,21 +406,94 @@
     return (3 * (256 + SIDES[branch]), width)
 
 
-def norm_kernel(gain, shift, out):
+def swap_blocks(parts):
+    rows = parts[0].shape[0]
+    group = lax.broadcasted_iota(jnp.int32, (rows, 128), 1) // 8
+    step = 1
+    while step < 16:
+        high = (group & step) != 0
+        parts = [
+            jnp.where(high, parts[i], pltpu.roll(parts[i - step], 128 - 8 * step, 1))
+            if i & step
+            else jnp.where(high, pltpu.roll(parts[i + step], 8 * step, 1), parts[i])
+            for i in range(16)
+        ]
+        step = 2 * step
+    return parts
+
+
+def joint_matrix():
+    source = lax.broadcasted_iota(jnp.int32, (256, 256), 0)
+    lane = lax.broadcasted_iota(jnp.int32, (256, 256), 1)
+    matches = (source // 8 == lane % C0) & (source % 8 == lane // C0) & (source < 136)
+    return jnp.where(matches, 1.0, 0.0)
+
+
+def shift_group(value, group):
+    return pltpu.roll(value, 128 - 8 * group, 1) if group else value
+
+
+def prepare_kernel(people, gain, shift, weight, bias, flip, targets, mask, *outs):
+    norms, weight_out, bias_out, flip_weight, flip_bias, target_out, mask_out, scratch = outs
     for base, ref in ((0, gain), (11, shift)):
         offset = 0
         line = base
         sizes = [channels for channels in CHANNELS for _ in range(2)] + [C0] * 3
         for channels in sizes:
             part = ref[0:1, offset : offset + channels]
-            out[line : line + 1, :] = jnp.concatenate([part] * (256 // channels), axis=1)
+            norms[line : line + 1, :] = jnp.concatenate([part] * (256 // channels), axis=1)
             offset += channels
             line += 1
+    joints = weight.shape[1]
+    source = lax.broadcasted_iota(jnp.int32, (joints, joints), 0)
+    moved = jnp.where(source == flip[...], 1.0, 0.0)
+    for matrix, row, matrix_out, row_out in (
+        (weight[...], bias[...], weight_out, bias_out),
+        (
+            jnp.dot(weight[...], moved, precision=lax.Precision.HIGHEST),
+            jnp.dot(bias[...], moved, precision=lax.Precision.HIGHEST),
+            flip_weight,
+            flip_bias,
+        ),
+    ):
+        matrix_out[...] = jnp.zeros((C0, C0), f32)
+        matrix_out[:, 0:joints] = matrix
+        row_out[...] = jnp.zeros((1, 256), f32)
+        for place in range(8):
+            row_out[0:1, C0 * place : C0 * place + joints] = row
+    lines = 2 * targets.shape[2]
+    parts = swap_blocks([targets[:, j].reshape(lines, 128) for j in range(16)])
+    last = targets[:, 16].reshape(lines, 128)
+    cells = mask[...].reshape(lines, 128).astype(f32)
+    lane = lax.broadcasted_iota(jnp.int32, (lines, 128), 1)
+    tails = [
+        jnp.where(lane < 8, shift_group(last, group), pltpu.roll(shift_group(cells, group), 8, 1))
+        for group in range(16)
+    ]
+    whole = jnp.concatenate(
+        [jnp.concatenate([part, tail], axis=1) for part, tail in zip(parts, tails)], axis=0
+    )
+    source = lax.broadcasted_iota(jnp.int32, (256, 256), 0)
+    target_lane = lax.broadcasted_iota(jnp.int32, (256, 256), 1)
+    spread = jnp.where((source >= 136) & (source < 144) & (source - 136 == target_lane // C0), 1.0, 0.0)
+    target_rows = dot_nn(whole, joint_matrix())
+    mask_rows = dot_nn(whole, spread)
+    first_image = lax.broadcasted_iota(jnp.int32, (lines, 256), 0) < lines // 2
+    share = jnp.where(first_image, people[0].astype(f32), people[1].astype(f32))
+    for value, ref in ((target_rows, target_out), (mask_rows, mask_out)):
+        for part in range(2):
+            for group in range(16):
+                span = slice(group * lines, (group + 1) * lines)
+                block = value[span, 128 * part : 128 * part + 128]
+                if ref is mask_out:
+                    block = block / share[:, :128]
+                scratch[pl.ds(group, lines, stride=16), :] = block
+            ref[:, 128 * part : 128 * part + 128] = scratch[...]
 
 
 def first_kernel(rows, packed, meta, *refs):
     xs, tops, bottoms, packs, tiles, mains, sums, taps, bands, sides, scratch = split_refs(
-        refs, 4, 1, 1, 4, 4, 4, 1, 7 * packed, 4, 4, 3 * packed
+        refs, 4, 1, 1, 2 if packed else 4, 4, 4, 1, 7 * packed, 4, 4, 3 * packed
     )
     sums = sums[0]
     if packed:
@@ -409,7 +545,7 @@
 
 def second_kernel(rows, counts, packed, meta, *refs):
     firsts, stat, norms, packs, outs, sums, taps, hidden, bands, sides, scratch = split_refs(
-        refs, 4, 1, 1, 4, 4, 1, 7 * packed, 4, 4, 4, 3 * packed
+        refs, 4, 1, 1, 2 if packed else 4, 4, 1, 7 * packed, 4, 4, 4, 3 * packed
     )
     sums = sums[0]
     if packed:
@@ -538,8 +674,8 @@
 
 
 def flip_kernel(rows, counts, *refs):
-    seconds, tiles, stat, unites, mix_stat, norms, weight, bias, heat, out = split_refs(
-        refs, 4, 4, 1, 6, 1, 1, 1, 1, 1, 1
+    seconds, tiles, stat, unites, mix_stat, norms, weight, bias, heat, out, scratch = split_refs(
+        refs, 4, 4, 1, 6, 1, 1, 1, 1, 1, 1, 2
     )
     stat, norms = stat[0], norms[0]
     mixes = []
@@ -554,7 +690,19 @@
             mixes.append(dot_nn(silu(value), mix_matrix(unite, branch)))
     pre = united_sum(base, mixes, mix_stat[0], norms, rows, counts)
     back = dot_nn(silu(pre), head_matrix(weight[0][...])) + bias[0][...]
-    out[0][...] = 0.5 * (heat[0][...] + back)
+    moved = dot_nt(0.5 * (heat[0][...] + back), joint_matrix())
+    scratch[0][...] = moved[:, :128]
+    scratch[1][...] = moved[:, 128:]
+    lines = 2 * rows[0]
+    parts = [scratch[0][pl.ds(group, lines, stride=16), :] for group in range(16)]
+    lane = lax.broadcasted_iota(jnp.int32, (lines, 128), 1)
+    last = None
+    for group in range(16):
+        tail = scratch[1][pl.ds(group, lines, stride=16), :]
+        tail = pltpu.roll(tail, 8 * group, 1) if group else tail
+        last = tail if last is None else jnp.where(lane // 8 == group, tail, last)
+    for joint, value in enumerate([*swap_blocks(parts), last]):
+        out[0][:, joint] = value.reshape(2, rows[0], 128)
 
 
 def edge_place(branch, image):
@@ -666,42 +814,33 @@
         write_edges(first, last, grad, branch, count, 0)
 
 
-def finish_grads(packed, meta, stage, unite_grads, outs, scratch):
-    if packed:
-        pack_grads(meta[2], stage, unite_grads, outs, scratch)
-    else:
-        for ref, value in zip(outs, stage):
-            ref[...] = value[...]
-
-
-def kernel_grad_second(rows, counts, packed, meta, *refs):
-    ins, unite_grads, outs, stage, scratch, hidden, sides, products = split_refs(
-        refs, 16, 3, 4, 5, 3, 4, 4, 4
-    )
-    grads, seconds, firsts = ins[0:4], ins[4:8], ins[8:12]
-    stat, stat_sums, first_stat, norms = ins[12:16]
-    for branch in range(4):
-        count, channels, total = rows[branch], CHANNELS[branch], counts[branch]
-        stats = moments(stat[2 * branch : 2 * branch + 2, :], channels, total)
-        grad = norm_input_grad(
-            grads[branch][...],
-            (seconds[branch][...] - stats[0]) * stats[1],
-            stats,
-            norms[2 * branch + 1 : 2 * branch + 2, :],
-            stat_sums[2 * branch : 2 * branch + 2, :],
-            channels,
-            total,
-        )
-        fill_hidden(meta, firsts, first_stat, norms, hidden, branch, count, total)
-        build_sides(hidden[branch], sides[branch], channels)
-        products[branch][...] = dot_tn(patches(hidden[branch], sides[branch], count), grad)
-        collect_band(products[branch], branch, tap_writer(stage[3 - branch], branch))
-    finish_grads(packed, meta, stage, unite_grads, outs, scratch)
+def kernel_grad_second(rows, counts, branch, meta, *refs):
+    grad, second, first, stat, stat_sums, first_stat, norms, out, hidden, side, product = refs
+    count, channels, total = rows[branch], CHANNELS[branch], counts[branch]
+    stats = moments(stat[2 * branch : 2 * branch + 2, :], channels, total)
+    value = norm_input_grad(
+        grad[...],
+        (second[...] - stats[0]) * stats[1],
+        stats,
+        norms[2 * branch + 1 : 2 * branch + 2, :],
+        stat_sums[2 * branch : 2 * branch + 2, :],
+        channels,
+        total,
+    )
+    fill_hidden(meta, {branch: first}, first_stat, norms, {branch: hidden}, branch, count, total)
+    build_sides(hidden, side, channels)
+    product[...] = dot_tn(patches(hidden, side, count), value)
+    collect_band(product, branch, tap_writer(out, branch))
+
+
+def pack_kernel(meta, *refs):
+    stage, unite_grads, outs, narrow, scratch = split_refs(refs, 4, 3, 2, 1, 3)
+    pack_grads(meta[2], [*stage, *narrow], unite_grads, outs, scratch)
 
 
 def kernel_grad_first(rows, counts, packed, meta, *refs):
     ins, unite_grads, outs, stage, scratch, sources, sides, products = split_refs(
-        refs, 15, 3, 4, 5, 3, 4, 4, 4
+        refs, 15, 3, 2 if packed else 4, 5, 3, 4, 4, 4
     )
     grads, firsts, tiles = ins[0:4], ins[4:8], ins[8:12]
     first_stat, first_sums, norms = ins[12:15]
@@ -721,7 +860,11 @@
         build_sides(sources[branch], sides[branch], channels)
         products[branch][...] = dot_tn(patches(sources[branch], sides[branch], count), grad)
         collect_band(products[branch], branch, tap_writer(stage[3 - branch], branch))
-    finish_grads(packed, meta, stage, unite_grads, outs, scratch)
+    if packed:
+        pack_grads(meta[2], stage, unite_grads, outs, scratch)
+    else:
+        for ref, value in zip(outs, stage):
+            ref[...] = value[...]
 
 
 def back_first_kernel(rows, counts, flags, *refs):
@@ -762,7 +905,15 @@
     def put(sums, line, channels):
         nonlocal offset
         for ref, row in ((shift, line), (gain, line + 1)):
-            ref[0:1, offset : offset + channels] = fold(sums[row : row + 1, :], channels)[:, :channels]
+            value = fold(sums[row : row + 1, :], channels)
+            done = 0
+            while done < channels:
+                place = offset + done
+                width = min(channels - done, 128 - place % 128)
+                ref[place // 128 : place // 128 + 1, place % 128 : place % 128 + width] = value[
+                    :, done : done + width
+                ]
+                done += width
         offset += channels
 
     for branch in range(4):
@@ -773,8 +924,10 @@
     loss[...] = jnp.sum(head_sums[6:7, :], axis=1, keepdims=True)
     joints = head_bias.shape[1]
     head_bias[...] = fold(head_sums[7:8, :], C0)[:, :joints]
-    for part in range(4):
-        head_weight[8 * part : 8 * part + 8, :] = head_sums[16:24, C0 * part : C0 * part + joints]
+    total = jnp.concatenate(
+        [head_sums[16:24, C0 * part : C0 * part + C0] for part in range(4)], axis=0
+    )
+    head_weight[...] = jnp.transpose(total)[:joints]
 
 
 def device_count():
@@ -785,10 +938,13 @@
     return lax.ppermute(value, AXES, [(i, i ^ bit) for i in range(device_count())])
 
 
-def total_sum(value, order=None):
+def total_sum(value, beside=()):
     value = value.value
-    for bit in order or [1 << i for i in range(device_count().bit_length() - 1)]:
-        value = value + exchange(value, bit)
+    for step in range(device_count().bit_length() - 1):
+        other = exchange(value, 1 << step)
+        if step < len(beside) and beside[step]:
+            other = after(other, beside[step](value))
+        value = value + other
     return Kept(value)
 
 
@@ -803,31 +959,51 @@
     return lax.axis_index("dp") * lax.axis_size("space") + lax.axis_index("space")
 
 
-def gather_halves(shard):
-    first_half = (device_index() & 16) == 0
-    other = exchange(shard, 16)
+def after(value, *others):
+    return lax.optimization_barrier((value, *others))[0]
+
+
+def swap(parts, step):
+    return [Kept(exchange(part.value, STEPS[chunk][step])) for chunk, part in enumerate(parts)]
+
+
+def gather_shards(meta, flat, beside):
+    other = exchange(flat, 16)
+    other = after(other, beside(flat))
+    shapes = [(1, 2, last - first, 128) for first, last in CHUNKS]
+    parts = call(split_shard, [meta, flat, Kept(other)], kept(shapes), smem=1)
+    shapes = [(2, *shape[1:]) for shape in shapes]
+    parts = call(join_chunks, [*parts, *swap(parts, 0)], kept(shapes))
+    shapes = [(4, *shape[2:]) for shape in shapes]
+    parts = call(join_apart, [*parts, *swap(parts, 1)], kept(shapes * 2))
     halves = []
-    for own in (jnp.where(first_half, shard, other), jnp.where(first_half, other, shard)):
-        far = exchange(own, 8)
-        packs = []
-        for cut, order in zip((slice(0, SPLIT), slice(SPLIT, SHARD)), GATHER_ORDER):
-            part = jnp.stack([own[cut], far[cut]])
-            for bit in order[1::-1]:
-                part = jnp.concatenate([part, exchange(part, bit)])
-            packs += [part, exchange(part, 1)]
-        halves.append(packs)
+    for half in (parts[:3], parts[3:]):
+        (whole,) = call(join_whole, [*half, *swap(half, 2)], kept([(8, SHARD, 128)]))
+        halves.append([whole, Kept(exchange(whole.value, 1))])
     return halves
 
 
-def scatter_half(packs):
-    parts = []
-    for keep, send, order in zip(packs[0::2], packs[1::2], SCATTER_ORDER):
-        value = keep + exchange(send, 1)
-        for bit in order:
-            half = value.shape[0] // 2
-            value = value[:half] + exchange(value[half:], bit)
-        parts.append(value[0])
-    return jnp.concatenate(parts)
+def scatter_shards(meta, packs, beside):
+    def both(count):
+        return kept([(count, 2, last - first, 128) for first, last in CHUNKS] * 2)
+
+    received = [Kept(exchange(send.value, 1)) for _, send in packs]
+    received[0] = Kept(after(received[0].value, beside[0](packs[0][1].value)))
+    parts = call(add_cores, [*[keep for keep, _ in packs], *received], both(4), cost=2)
+    for step in range(3):
+        received = swap(parts[3:], step)
+        if beside[1 + step]:
+            received[0] = Kept(after(received[0].value, beside[1 + step](parts[3].value)))
+        if step < 2:
+            parts = call(add_received, [*parts[:3], *received], both(2 - step))
+        else:
+            keep, send = call(
+                add_last, [meta, *parts[:3], *received], kept([(SHARD, 128)] * 2), smem=1
+            )
+    received = exchange(send.value, 16)
+    received = after(received, beside[4](send.value))
+    shapes = [(ROWS_THREE, 128), (ROWS_TWO, 128), (ROWS_ONE, 128), (8, 128)]
+    return call(add_shard, [keep, Kept(received)], shapes)
 
 
 def body(
@@ -865,11 +1041,43 @@
     shards_in = (convs_three, convs_two, convs_one, convs_zero, unite_one, unite_two, unite_three)
     sizes = [part.shape[0] for part in shards_in]
 
+    meta = jnp.stack(
+        [place > 0, place < spaces - 1, device_index() & 15, (device_index() & 16) // 16]
+    ).astype(jnp.int32)
+
+    state = {}
+
+    def prepare(start):
+        parts = lax.optimization_barrier((*inputs, start))[:4]
+        last_rows = jnp.concatenate([value[:, -2:] for value in parts], axis=1)
+        first_rows = jnp.concatenate([value[:, :2] for value in parts], axis=1)
+        state["halo"] = move_rows(first_rows, last_rows)
+        state["small"] = call(
+            prepare_kernel,
+            [
+                after(person_count, start),
+                norm_gain[None],
+                norm_shift[None],
+                head_weight,
+                head_bias[None],
+                flip_order[None],
+                targets,
+                crowd_mask,
+            ],
+            kept([(22, 256), (C0, C0), (1, 256), (C0, C0), (1, 256)] + [(cells[0], 256)] * 2),
+            [(cells[0], 128)],
+            smem=1,
+            cost=5,
+        )
+        return state["small"][0].value
+
     if packed:
         gap = jnp.zeros(((24 - ROWS_ONE) * 128,), f32)
-        flat = jnp.concatenate([*shards_in[:3], gap, *shards_in[3:]])
-        first_packs, second_packs = gather_halves(flat.reshape(SHARD, 128))
+        flat = jnp.concatenate([*shards_in[:3], gap, *shards_in[3:]]).reshape(SHARD, 128)
+        first_packs, second_packs = gather_shards(meta, flat, prepare)
+        first_meta = after(meta, second_packs[0].value)
     else:
+        prepare(meta)
         whole = [lax.all_gather(part, AXES, axis=0, tiled=True) for part in shards_in]
         whole = [
             part.reshape(-1, width)
@@ -877,34 +1085,9 @@
         ]
         first_packs = [part[: part.shape[0] // 2] for part in whole]
         second_packs = [part[part.shape[0] // 2 :] for part in whole]
-
-    last_rows = jnp.concatenate([value[:, -2:] for value in inputs], axis=1)
-    first_rows = jnp.concatenate([value[:, :2] for value in inputs], axis=1)
-    tops, bottoms = move_rows(first_rows, last_rows)
-    meta = jnp.stack([place > 0, place < spaces - 1, device_index() & 15]).astype(jnp.int32)
-
-    (norms,) = call(norm_kernel, [norm_gain[None], norm_shift[None]], kept([(22, 256)]), limit=4)
-
-    def head_parts(weight, bias):
-        weight = jnp.pad(weight, ((0, 0), (0, C0 - joints)))
-        bias = jnp.tile(jnp.pad(bias, (0, C0 - joints)), 8)[None]
-        return weight, bias
-
-    weight, bias = head_parts(head_weight, head_bias)
-    flip_weight, flip_bias = head_parts(head_weight[:, flip_order], head_bias[flip_order])
-    target_cells = jnp.pad(
-        jnp.transpose(targets.reshape(2, joints, rows[0], 16, 8), (0, 2, 3, 4, 1)),
-        ((0, 0),) * 4 + ((0, C0 - joints),),
-    ).reshape(cells[0], 256)
-    loss_weight = crowd_mask.astype(f32) / person_count.astype(f32)[:, None, None]
-    loss_weight = jnp.broadcast_to(
-        loss_weight.reshape(2, rows[0], 16, 8, 1), (2, rows[0], 16, 8, C0)
-    ).reshape(cells[0], 256)
-    first_meta, weight, bias, flip_weight, flip_bias, target_cells, loss_weight = (
-        lax.optimization_barrier(
-            (meta, weight, bias, flip_weight, flip_bias, target_cells, loss_weight)
-        )
-    )
+        first_meta = meta
+    tops, bottoms = state["halo"]
+    norms, weight, bias, flip_weight, flip_bias, target_cells, loss_weight = state["small"]
 
     bands = [band_shape(b, 256) for b in range(4)]
     inner = [(cells[b], 256) for b in range(4)]
@@ -1021,27 +1204,34 @@
     )
     normed_grads = out[0:4]
     above, below = move_rows(out[5], out[6])
-    first_sums = total_sum(out[4])
-
-    grads_out = list(PACKS) if packed else list(TAPS_OUT[:4])
-    second_kernels = call(
-        functools.partial(kernel_grad_second, rows, counts, packed),
-        [
-            meta,
-            *join_grads,
-            *seconds,
-            *firsts,
-            second_stat,
-            second_sums,
-            first_stat,
-            norms,
-            *second_mixers,
-        ],
-        grads_out,
-        [*STAGE, *PACK_SCRATCH] + wide + sides_of(wide) + bands,
-        smem=1,
-        cost=8,
-    )
+    stage = [None] * 4
+
+    def second_grad(branch):
+        def work(start):
+            stage[3 - branch] = call(
+                functools.partial(kernel_grad_second, rows, counts, branch),
+                [
+                    after(meta, start),
+                    join_grads[branch],
+                    seconds[branch],
+                    firsts[branch],
+                    second_stat,
+                    second_sums,
+                    first_stat,
+                    norms,
+                ],
+                kept([TAPS_OUT[3 - branch]]),
+                [wide[branch], sides_of(wide)[branch], bands[branch]],
+                smem=1,
+                cost=2,
+            )[0]
+            return stage[3 - branch].value
+
+        return work
+
+    first_sums = total_sum(out[4], [None] + [second_grad(branch) for branch in range(4)])
+
+    grads_out = kept([(8, SHARD, 128)] * 2) if packed else list(TAPS_OUT[:4])
     first_kernels = call(
         functools.partial(kernel_grad_first, rows, counts, packed),
         [
@@ -1059,102 +1249,114 @@
         smem=1,
         cost=7,
     )
+    def back_first(start):
+        state["source"] = call(
+            functools.partial(back_first_kernel, rows, counts),
+            [
+                after(meta, start),
+                *normed_grads,
+                *firsts,
+                *join_grads,
+                *first_taps,
+                above,
+                below,
+                first_stat,
+                first_sums,
+                norms,
+            ],
+            [value.shape for value in inputs],
+            wide + sides_of(wide) + bands,
+            smem=1,
+            cost=7,
+        )
+        return state["source"][0]
+
+    def flip_first(start):
+        state["firsts"] = call(
+            functools.partial(first_flip_kernel, rows),
+            [after(meta, start), *tiles, *first_taps],
+            kept(wide),
+            bands + sides_of(wider),
+            smem=1,
+            cost=6,
+        )
+        return state["firsts"][0].value
+
+    def flip_second(start):
+        state["seconds"] = call(
+            functools.partial(second_flip_kernel, rows, counts),
+            [after(meta, start), *state["firsts"], first_stat, norms, *second_taps],
+            kept(inner),
+            wide + bands + sides_of(wide),
+            smem=1,
+            cost=6,
+        )
+        return state["seconds"][0].value
+
+    def flip_last(start):
+        (state["heat"],) = call(
+            functools.partial(flip_kernel, rows, counts),
+            [
+                *state["seconds"],
+                *tiles,
+                second_stat,
+                *unites,
+                mix_stat,
+                norms,
+                flip_weight,
+                Kept(after(flip_bias.value, start)),
+                heat,
+            ],
+            [targets.shape],
+            [(cells[0], 128)] * 2,
+            cost=5,
+        )
+        return state["heat"]
+
     if packed:
-        second_part = scatter_half(second_kernels)
-        first_part = scatter_half(first_kernels)
-
-    source_grads = call(
-        functools.partial(back_first_kernel, rows, counts),
-        [
-            meta,
-            *normed_grads,
-            *firsts,
-            *join_grads,
-            *first_taps,
-            above,
-            below,
-            first_stat,
-            first_sums,
-            norms,
-        ],
-        [value.shape for value in inputs],
-        wide + sides_of(wide) + bands,
-        smem=1,
-        cost=7,
-    )
-
-    late_meta, _ = lax.optimization_barrier((meta, first_sums.value))
-    flip_firsts = call(
-        functools.partial(first_flip_kernel, rows),
-        [late_meta, *tiles, *first_taps],
-        kept(wide),
-        bands + sides_of(wider),
-        smem=1,
-        cost=6,
-    )
-    flip_seconds = call(
-        functools.partial(second_flip_kernel, rows, counts),
-        [late_meta, *flip_firsts, first_stat, norms, *second_taps],
-        kept(inner),
-        wide + bands + sides_of(wide),
-        smem=1,
-        cost=6,
-    )
-    (heat_mean,) = call(
-        functools.partial(flip_kernel, rows, counts),
-        [
-            *flip_seconds,
-            *tiles,
-            second_stat,
-            *unites,
-            mix_stat,
-            norms,
-            flip_weight,
-            flip_bias,
-            heat,
-        ],
-        [inner[0]],
-        cost=2,
-    )
-
-    if packed:
-        first_half = (device_index() & 16) == 0
-        shard = jnp.where(first_half, first_part, second_part)
-        shard = shard + exchange(jnp.where(first_half, second_part, first_part), 16)
-        top = ROWS_THREE + ROWS_TWO + ROWS_ONE
-        shard = jnp.concatenate([shard[:top].reshape(-1), shard[-8:].reshape(-1)])
-        shards, offset = [], 0
-        for size in sizes:
-            shards.append(shard[offset : offset + size])
+        second_kernels = call(
+            pack_kernel,
+            [after(meta, first_sums.value), *stage, *second_mixers],
+            grads_out,
+            [STAGE[4], *PACK_SCRATCH],
+            smem=1,
+        )
+        shard_parts = scatter_shards(
+            meta, (first_kernels, second_kernels), (flip_first, back_first, flip_second, None, flip_last)
+        )
+        rest, offset, shards = shard_parts[3].reshape(-1), 0, []
+        for size in sizes[3:]:
+            shards.append(rest[offset : offset + size])
             offset += size
+        shards = [*[part.reshape(-1) for part in shard_parts[:3]], *shards]
     else:
+        for work in (flip_first, back_first, flip_second, flip_last):
+            work(first_sums.value)
+        stage = [part.value for part in stage]
         flat = [
             jnp.concatenate([one.reshape(-1), two.reshape(-1)])
-            for one, two in zip([*first_kernels, *first_mixers], [*second_kernels, *second_mixers])
+            for one, two in zip([*first_kernels, *first_mixers], [*stage, *second_mixers])
         ]
         shards = [lax.psum_scatter(part, AXES, scatter_dimension=0, tiled=True) for part in flat]
 
     gain_grad, shift_grad, loss, head_grad, bias_grad = call(
         finish_kernel,
         [first_sums, second_sums, head_sums],
-        [norm_gain[None].shape, norm_shift[None].shape, (1, 1), head_weight.shape, (1, joints)],
+        [(9, 128), (9, 128), (1, 1), (joints, C0), (1, joints)],
         limit=4,
     )
-    heat_mean = jnp.transpose(
-        heat_mean.reshape(2, rows[0], 16, 8, C0)[..., :joints], (0, 4, 1, 2, 3)
-    ).reshape(targets.shape)
     return (
         loss[0, 0],
-        heat_mean,
-        *source_grads,
+        state["heat"],
+        *state["source"],
         shards[3],
         shards[2],
         shards[1],
         shards[0],
         *shards[4:7],
-        gain_grad[0],
-        shift_grad[0],
-        head_grad,
+        gain_grad.reshape(-1)[: norm_gain.shape[0]],
+        shift_grad.reshape(-1)[: norm_shift.shape[0]],
+        jnp.transpose(head_grad),
         bias_grad[0],
     )
 

time: 352 us -> 270 us (0.77)
  local copies, waits for them, and re-layouts: 54.1 us -> 15.3 us
  waiting for transfers between devices: 130 us -> 91.2 us
  other arithmetic: 14.1 us -> 0.44 us
  starting transfers between devices: 72.5 us -> 80.6 us
    ppermute x62 -> x57, waiting for transfers between devices: 128 us -> 87 us  [exchange(): lax.ppermute(value, AXES, [(i, i ^ bit) for i in range(device_count())])]
    reshape x5 -> x0, local copies, waits for them, and re-layouts: 14.4 us -> none  [the longest x1 4.18 us: body(): loss_weight = jnp.broadcast_to(loss_weight.reshape(2, rows[0], 16, 8, 1),...]
    add x43 -> x30, other arithmetic: 8.47 us -> 0.11 us  [total_sum(): value = value + other]
    ppermute x62 -> x57, starting transfers between devices: 62.6 us -> 70.3 us  [exchange(): lax.ppermute(value, AXES, [(i, i ^ bit) for i in range(device_count())])]
    unnamed x87 -> x25, local copies, waits for them, and re-layouts: 11.4 us -> 4.78 us
    pad x5 -> x0, local copies, waits for them, and re-layouts: 6.64 us -> none  [the longest x1 4.76 us: body(): jnp.pad(jnp.transpose(targets.reshape(2, joints, rows[0], 16, 8), (0, 2,...]
    slice x23 -> x8, local copies, waits for them, and re-layouts: 9.63 us -> 6.98 us  [the longest x3 3.72 us: body(): shards.append(rest[offset:offset + size])]
    pallas_call x14 -> x28, Pallas kernels: 74.4 us -> 76.2 us  [call(): pl.pallas_call(kernel, in_specs=specs, out_specs=[pl.BlockSpec(memory_spa...]
  transfers between devices with their start and end apart: 68 -> 63, of which waited for: 46 -> 44; matrix products, arithmetic and copies ran while one was open for 17% -> 3% of each run, Pallas kernels for 15% -> 18%
where the time goes in v1:
time: 270 us; the launch traced here: 265 us
  waiting for transfers between devices  91.2 us (34%)
  starting transfers between devices  80.6 us (30%)
  Pallas kernels  76.2 us (28%)
  local copies, waits for them, and re-layouts  15.3 us (6%)
    ppermute x57, waiting for transfers between devices, exchange(): lax.ppermute(value, AXES, [(i, i ^ bit) for i in range(device_count())])  87 us
    pallas_call x28, Pallas kernels, call(): pl.pallas_call(kernel, in_specs=specs, out_specs=[pl.BlockSpec(memory_spa...  76.2 us
    ppermute x57, starting transfers between devices, exchange(): lax.ppermute(value, AXES, [(i, i ^ bit) for i in range(device_count())])  70.3 us
    ppermute x6, starting transfers between devices, move_rows(): return (lax.ppermute(last, 'space', down), lax.ppermute(first, 'space', up))  10.4 us
  transfers between devices with their start and end apart: 63, of which 44 were waited for; matrix products, arithmetic and copies ran while one was open for 3% of the time, Pallas kernels for 18%

profile of v1, /device:TPU:0, one launch (start us, length us, event | category | flops | bytes accessed | tf_op | source)
XLA Modules:
  0.0 265.2 jit_solution(4328813544259730735)
XLA Ops:
  1.7 4.0 %collective-permute-start = (f32[392,128]{1,0:T(8,128)S(1)}, f32[392,128]{1,0:T(8,128)S(1)}, u32[]{:S(2)}, u32[]{:S(2)}) collective-permute-start(f32[392,128]{1,0:T(8,128)S(1)} %bitcast.23), channel_id=1, source_target_pairs={{0,16},{1,17},{2,18},{3,19},{4,20},{5,21},{6,22},{7,23},{8,24},{9,... | collective-permute-start | bytes 602120 | tf_op jit(solution)/shard_map/ppermute | solution.py:938
  10.3 3.4 %shard_map.314 = (f32[22,256]{1,0:T(8,128)S(1)}, f32[32,32]{1,0:T(8,128)S(1)}, f32[1,256]{1,0:T(1,128)S(1)}, f32[32,32]{1,0:T(8,128)S(1)}, f32[1,256]{1,0:T(1,12...) custom-call(s32[2]{0:T(128)S(1)} %copy-done, f32[1,1056]{1,0:T(1,128)} %broadcast_in_dim.16.gain, ...), custom_call_target="tpu_custom_call" | custom-call | flops 5500000256 | bytes 15000000 | tf_op jit(solution)/shard_map/pallas_call | solution.py:391
  26.7 4.4 %collective-permute-done.4.refs_3_ = f32[2,2,128,128]{3,2,1,0:T(8,128)S(1)} collective-permute-done((f32[2,2,128,128]{3,2,1,0:T(8,128)S(1)}, f32[2,2,128,128]{3,2,1,0:T(8,128)S(1)}, u32[]{:S(2)}, u32[]{:S(2)}) %collective-permute-start.4) | collective-permute-done | bytes 262176 | tf_op jit(solution)/shard_map/ppermute | solution.py:938
  44.4 3.1 %collective-permute-done.9.refs_5_ = f32[4,136,128]{2,1,0:T(8,128)S(1)} collective-permute-done((f32[4,136,128]{2,1,0:T(8,128)S(1)}, f32[4,136,128]{2,1,0:T(8,128)S(1)}, u32[]{:S(2)}, u32[]{:S(2)}) %collective-permute-start.9) | collective-permute-done | bytes 278560 | tf_op jit(solution)/shard_map/ppermute | solution.py:938
  54.6 7.6 %shard_map.320 = (f32[2,576,256]{2,1,0:T(8,128)S(1)}, f32[2,320,256]{2,1,0:T(8,128)S(1)}, f32[2,192,256]{2,1,0:T(8,128)S(1)}, f32[2,128,256]{2,1,0:T(8,128)S(1)}...) custom-call(s32[4]{0:T(128)S(1)} %pad_add_fusion.meta.flags, ...), custom_call_target="tpu_custom_call" | custom-call | flops 7699999744 | bytes 21000000 | tf_op jit(solution)/shard_map/pallas_call | solution.py:391
  62.2 4.8 %collective-permute-start.16 = (f32[8,256]{1,0:T(8,128)S(1)}, f32[8,256]{1,0:T(8,128)S(1)}, u32[]{:S(2)}, u32[]{:S(2)}) collective-permute-start(f32[8,256]{1,0:T(8,128)S(1)} %get-tuple-element.183), channel_id=1, source_target_pairs={{0,1},{1,0},{2,3},{3,2},{4,5},{5,4},{6,7},{7,6},{8,9},{9,8},{10,11... | collective-permute-start | bytes 24584 | tf_op jit(solution)/shard_map/ppermute | solution.py:938
  68.0 3.6 %collective-permute-done.17 = f32[8,256]{1,0:T(8,128)S(1)} collective-permute-done((f32[8,256]{1,0:T(8,128)S(1)}, f32[8,256]{1,0:T(8,128)S(1)}, u32[]{:S(2)}, u32[]{:S(2)}) %collective-permute-start.17) | collective-permute-done | bytes 8224 | tf_op jit(solution)/shard_map/ppermute | solution.py:938
  78.9 3.0 %collective-permute-start.20 = (f32[8,256]{1,0:T(8,128)S(1)}, f32[8,256]{1,0:T(8,128)S(1)}, u32[]{:S(2)}, u32[]{:S(2)}) collective-permute-start(f32[8,256]{1,0:T(8,128)S(1)} %add.99), channel_id=1, source_target_pairs={{0,16},{1,17},{2,18},{3,19},{4,20},{5,21},{6,22},{7,23},{8,24},{9,... | collective-permute-start | bytes 24584 | tf_op jit(solution)/shard_map/ppermute | solution.py:938
  83.4 7.0 %shard_map.321 = (f32[1024,256]{1,0:T(8,128)S(1)}, f32[512,256]{1,0:T(8,128)S(1)}, f32[256,256]{1,0:T(8,128)S(1)}, f32[128,256]{1,0:T(8,128)S(1)}, f32[8,256]{1,...) custom-call(s32[4]{0:T(128)S(1)} %pad_add_fusion.meta.flags, ...), custom_call_target="tpu_custom_call" | custom-call | flops 7699999744 | bytes 21000000 | tf_op jit(solution)/shard_map/pallas_call | solution.py:391
  91.7 3.6 %collective-permute-done.23 = f32[8,256]{1,0:T(8,128)S(1)} collective-permute-done((f32[8,256]{1,0:T(8,128)S(1)}, f32[8,256]{1,0:T(8,128)S(1)}, u32[]{:S(2)}, u32[]{:S(2)}) %collective-permute-start.23) | collective-permute-done | bytes 8224 | tf_op jit(solution)/shard_map/ppermute | solution.py:938
  109.4 3.6 %collective-permute-done.28 = f32[8,256]{1,0:T(8,128)S(1)} collective-permute-done((f32[8,256]{1,0:T(8,128)S(1)}, f32[8,256]{1,0:T(8,128)S(1)}, u32[]{:S(2)}, u32[]{:S(2)}) %collective-permute-start.28) | collective-permute-done | bytes 8224 | tf_op jit(solution)/shard_map/ppermute | solution.py:938
  128.8 3.8 %collective-permute-done.33 = f32[24,256]{1,0:T(8,128)S(1)} collective-permute-done((f32[24,256]{1,0:T(8,128)S(1)}, f32[24,256]{1,0:T(8,128)S(1)}, u32[]{:S(2)}, u32[]{:S(2)}) %collective-permute-start.33) | collective-permute-done | bytes 24608 | tf_op jit(solution)/shard_map/ppermute | solution.py:938
  148.6 3.6 %collective-permute-done.40 = f32[8,256]{1,0:T(8,128)S(1)} collective-permute-done((f32[8,256]{1,0:T(8,128)S(1)}, f32[8,256]{1,0:T(8,128)S(1)}, u32[]{:S(2)}, u32[]{:S(2)}) %collective-permute-start.40) | collective-permute-done | bytes 8224 | tf_op jit(solution)/shard_map/ppermute | solution.py:938
  169.0 7.0 %shard_map.325 = (f32[1024,256]{1,0:T(8,128)S(1)}, f32[512,256]{1,0:T(8,128)S(1)}, f32[256,256]{1,0:T(8,128)S(1)}, f32[128,256]{1,0:T(8,128)S(1)}, f32[8,256]{1,...) custom-call(s32[4]{0:T(128)S(1)} %pad_add_fusion.meta.flags, ...), custom_call_target="tpu_custom_call" | custom-call | flops 7699999744 | bytes 21000000 | tf_op jit(solution)/shard_map/pallas_call | solution.py:391
  176.0 4.8 %collective-permute-start.44 = (f32[8,256]{1,0:T(8,128)S(1)}, f32[8,256]{1,0:T(8,128)S(1)}, u32[]{:S(2)}, u32[]{:S(2)}) collective-permute-start(f32[8,256]{1,0:T(8,128)S(1)} %get-tuple-element.222), channel_id=1, source_target_pairs={{0,1},{1,0},{2,3},{3,2},{4,5},{5,4},{6,7},{7,6},{8,9},{9,8},{10,11... | collective-permute-start | bytes 24584 | tf_op jit(solution)/shard_map/ppermute | solution.py:938
  181.8 3.6 %shard_map.326.refs_3_ = f32[288,32]{1,0:T(8,128)S(1)} custom-call(s32[4]{0:T(128)S(1)} %pad_add_fusion.meta.flags, f32[1024,256]{1,0:T(8,128)S(1)} %get-tuple-element.207.refs_13_.refs_0_.refs_8_, f32[1024,256]{1,0:T(8,128)S(1)} %get-tuple-element.184.refs_0_.refs_6_.refs_4_.refs_1_, f32[2,544,256]{2,1,0:T(8,128)S(1)} %get-tuple-element.179.refs_0_.refs_8_.refs_2_.refs_4_, ...), custom_call_target="tpu_custom_call" | custom-call | flops 2200000000 | bytes 6000000 | tf_op jit(solution)/shard_map/pallas_call | solution.py:391
  197.3 6.4 %shard_map.331 = (f32[8,392,128]{2,1,0:T(8,128)S(1)}, f32[8,392,128]{2,1,0:T(8,128)S(1)}) custom-call(s32[4]{0:T(128)S(1)} %pad_add_fusion.meta.flags, f32[1024,256]{1,0:T(8,128)S(1)} %get-tuple-element.232.refs_0_, f32[512,256]{1,0:T(8,128)S(1)} %get-tuple-element.233.refs_1_, f32[256,256]{1,0:T(8,128)S(1)} %get-tuple-element.234.refs_2_, ...), custom_call_target="tpu_custom_call" | custom-call | flops 7699999744 | bytes 21000000 | tf_op jit(solution)/shard_map/pallas_call | solution.py:391
  209.9 5.7 %shard_map.333 = (f32[2,544,256]{2,1,0:T(8,128)S(1)}, f32[2,288,256]{2,1,0:T(8,128)S(1)}, f32[2,160,256]{2,1,0:T(8,128)S(1)}, f32[2,96,256]{2,1,0:T(8,128)S(1)}) custom-call(s32[4]{0:T(128)S(1)} %pad_add_fusion.meta.flags, f32[2,576,256]{2,1,0:T(8,128)S(1)} %get-tuple-element.185.refs_1_.refs_8_.refs_0_.refs_4_, ...), custom_call_target="tpu_custom_call" | custom-call | flops 6600000000 | bytes 18000000 | tf_op jit(solution)/shard_map/pallas_call | solution.py:391
  218.1 4.2 %collective-permute-start.55 = (f32[4,2,136,128]{3,2,1,0:T(8,128)S(1)}, f32[4,2,136,128]{3,2,1,0:T(8,128)S(1)}, u32[]{:S(2)}, u32[]{:S(2)}) collective-permute-start(f32[4,2,136,128]{3,2,1,0:T(8,128)S(1)} %get-tuple-element.261), channel_id=1, source_target_pairs={{0,2},{1,3},{2,0},{3,1},{4,6},{5,7},{6,4},{7,5},{8,10},{9,11},{10,... | collective-permute-start | bytes 1671176 | tf_op jit(solution)/shard_map/ppermute | solution.py:938
  223.6 7.2 %shard_map.335 = (f32[2,32,4096]{2,1,0:T(8,128)}, f32[2,16,4096]{2,1,0:T(8,128)}, f32[2,8,4096]{2,1,0:T(8,128)}, f32[2,4,4096]{2,1,0:T(4,128)}) custom-call(s32[4]{0:T(128)S(1)} %pad_add_fusion.meta.flags, f32[1024,256]{1,0:T(8,128)S(1)} %get-tuple-element.232.refs_0_, f32[512,256]{1,0:T(8,128)S(1)} %get-tuple-element.233.refs_1_, ...), custom_call_target="tpu_custom_call" | custom-call | flops 7699999744 | bytes 21000000 | tf_op jit(solution)/shard_map/pallas_call | solution.py:391
  230.8 3.9 %collective-permute-done.55.refs_5_ = f32[4,2,136,128]{3,2,1,0:T(8,128)S(1)} collective-permute-done((f32[4,2,136,128]{3,2,1,0:T(8,128)S(1)}, f32[4,2,136,128]{3,2,1,0:T(8,128)S(1)}, u32[]{:S(2)}, u32[]{:S(2)}) %collective-permute-start.55) | collective-permute-done | bytes 557088 | tf_op jit(solution)/shard_map/ppermute | solution.py:938
  237.3 6.1 %shard_map.337 = (f32[1024,256]{1,0:T(8,128)S(1)}, f32[512,256]{1,0:T(8,128)S(1)}, f32[256,256]{1,0:T(8,128)S(1)}, f32[128,256]{1,0:T(8,128)S(1)}) custom-call(s32[4]{0:T(128)S(1)} %pad_add_fusion.meta.flags, f32[2,544,256]{2,1,0:T(8,128)S(1)} %get-tuple-element.248.refs_0_, f32[2,288,256]{2,1,0:T(8,128)S(1)} %get-tuple-element.264.refs_1_, ...), custom_call_target="tpu_custom_call" | custom-call | flops 6600000000 | bytes 18000000 | tf_op jit(solution)/shard_map/pallas_call | solution.py:391
  252.6 4.3 %shard_map.340 = f32[2,17,32,128]{3,2,1,0:T(8,128)} custom-call(f32[1024,256]{1,0:T(8,128)S(1)} %get-tuple-element.267.refs_0_, f32[512,256]{1,0:T(8,128)S(1)} %get-tuple-element.268.refs_1_, f32[256,256]{1,0:T(8,128)S(1)} %get-tuple-element.269.refs_2_, f32[128,256]{1,0:T(8,128)S(1)} %get-tuple-element.270.refs_3_, ...), custom_call_target="tpu_custom_call" | custom-call | flops 5500000256 | bytes 15000000 | tf_op jit(solution)/shard_map/pallas_call | solution.py:391
  256.9 3.7 %collective-permute-done.62.received = f32[392,128]{1,0:T(8,128)S(1)} collective-permute-done((f32[392,128]{1,0:T(8,128)S(1)}, f32[392,128]{1,0:T(8,128)S(1)}, u32[]{:S(2)}, u32[]{:S(2)}) %collective-permute-start.62) | collective-permute-done | bytes 200736 | tf_op jit(solution)/shard_map/ppermute | solution.py:938
  (202 shorter events, 151.7 us)
Async XLA Ops:
  1.7 13.3 %collective-permute-start = (f32[392,128]{1,0:T(8,128)S(1)}, f32[392,128]{1,0:T(8,128)S(1)}, u32[]{:S(2)}, u32[]{:S(2)}) collective-permute-start(f32[392,128]{1,0:T(8,128)S(1)} %bitcast.23), channel_id=1, source_target_pairs={{0,16},{1,17},{2,18},{3,19},{4,20},{5,21},{6,22},{7,23},{8,24},{9,... | collective-permute-start | bytes 602120 | tf_op jit(solution)/shard_map/ppermute | solution.py:938
  16.0 7.3 %collective-permute-start.3 = (f32[1,2,136,128]{3,2,1,0:T(8,128)S(1)}, f32[1,2,136,128]{3,2,1,0:T(8,128)S(1)}, u32[]{:S(2)}, u32[]{:S(2)}) collective-permute-start(f32[1,2,136,128]{3,2,1,0:T(8,128)S(1)} %get-tuple-element.164.refs_2_), channel_id=1, source_target_pairs={{0,2},{1,3},{2,0},{3,1},{4,6},{5,7},{6,4},{7,5},{8,10},{9,11},{10,... | collective-permute-start | bytes 417800 | tf_op jit(solution)/shard_map/ppermute | solution.py:938
  23.3 10.2 %collective-permute-start.6 = (f32[2,2,136,128]{3,2,1,0:T(8,128)S(1)}, f32[2,2,136,128]{3,2,1,0:T(8,128)S(1)}, u32[]{:S(2)}, u32[]{:S(2)}) collective-permute-start(f32[2,2,136,128]{3,2,1,0:T(8,128)S(1)} %get-tuple-element.167.refs_2_), channel_id=1, source_target_pairs={{0,8},{1,9},{2,10},{3,11},{4,12},{5,13},{6,14},{7,15},{8,0},{9,1},... | collective-permute-start | bytes 835592 | tf_op jit(solution)/shard_map/ppermute | solution.py:938
  26.2 7.3 %collective-permute-start.5 = (f32[2,2,128,128]{3,2,1,0:T(8,128)S(1)}, f32[2,2,128,128]{3,2,1,0:T(8,128)S(1)}, u32[]{:S(2)}, u32[]{:S(2)}) collective-permute-start(f32[2,2,128,128]{3,2,1,0:T(8,128)S(1)} %get-tuple-element.166.refs_1_), channel_id=1, source_target_pairs={{0,2},{1,3},{2,0},{3,1},{4,6},{5,7},{6,4},{7,5},{8,10},{9,11},{10,... | collective-permute-start | bytes 786440 | tf_op jit(solution)/shard_map/ppermute | solution.py:938
  33.6 7.4 %collective-permute-start.12 = (f32[4,128,128]{2,1,0:T(8,128)S(1)}, f32[4,128,128]{2,1,0:T(8,128)S(1)}, u32[]{:S(2)}, u32[]{:S(2)}) collective-permute-start(f32[4,128,128]{2,1,0:T(8,128)S(1)} %get-tuple-element.176.refs_0_), channel_id=1, source_target_pairs={{0,2},{1,3},{2,0},{3,1},{4,6},{5,7},{6,4},{7,5},{8,10},{9,11},{10,... | collective-permute-start | bytes 786440 | tf_op jit(solution)/shard_map/ppermute | solution.py:938
  33.9 8.0 %collective-permute-start.13 = (f32[4,128,128]{2,1,0:T(8,128)S(1)}, f32[4,128,128]{2,1,0:T(8,128)S(1)}, u32[]{:S(2)}, u32[]{:S(2)}) collective-permute-start(f32[4,128,128]{2,1,0:T(8,128)S(1)} %get-tuple-element.177.refs_1_), channel_id=1, source_target_pairs={{0,8},{1,9},{2,10},{3,11},{4,12},{5,13},{6,14},{7,15},{8,0},{9,1},... | collective-permute-start | bytes 786440 | tf_op jit(solution)/shard_map/ppermute | solution.py:938
  34.0 9.2 %collective-permute-start.14 = (f32[4,136,128]{2,1,0:T(8,128)S(1)}, f32[4,136,128]{2,1,0:T(8,128)S(1)}, u32[]{:S(2)}, u32[]{:S(2)}) collective-permute-start(f32[4,136,128]{2,1,0:T(8,128)S(1)} %get-tuple-element.178.refs_2_), channel_id=1, source_target_pairs={{0,4},{1,5},{2,6},{3,7},{4,0},{5,1},{6,2},{7,3},{8,12},{9,13},{10,... | collective-permute-start | bytes 835592 | tf_op jit(solution)/shard_map/ppermute | solution.py:938
  35.8 8.1 %collective-permute-start.7 = (f32[4,128,128]{2,1,0:T(8,128)S(1)}, f32[4,128,128]{2,1,0:T(8,128)S(1)}, u32[]{:S(2)}, u32[]{:S(2)}) collective-permute-start(f32[4,128,128]{2,1,0:T(8,128)S(1)} %get-tuple-element.168.refs_0_), channel_id=1, source_target_pairs={{0,2},{1,3},{2,0},{3,1},{4,6},{5,7},{6,4},{7,5},{8,10},{9,11},{10,... | collective-permute-start | bytes 786440 | tf_op jit(solution)/shard_map/ppermute | solution.py:938
  37.4 7.1 %collective-permute-start.8 = (f32[4,128,128]{2,1,0:T(8,128)S(1)}, f32[4,128,128]{2,1,0:T(8,128)S(1)}, u32[]{:S(2)}, u32[]{:S(2)}) collective-permute-start(f32[4,128,128]{2,1,0:T(8,128)S(1)} %get-tuple-element.169.refs_1_), channel_id=1, source_target_pairs={{0,8},{1,9},{2,10},{3,11},{4,12},{5,13},{6,14},{7,15},{8,0},{9,1},... | collective-permute-start | bytes 786440 | tf_op jit(solution)/shard_map/ppermute | solution.py:938
  41.0 6.5 %collective-permute-start.9 = (f32[4,136,128]{2,1,0:T(8,128)S(1)}, f32[4,136,128]{2,1,0:T(8,128)S(1)}, u32[]{:S(2)}, u32[]{:S(2)}) collective-permute-start(f32[4,136,128]{2,1,0:T(8,128)S(1)} %get-tuple-element.170.refs_2_), channel_id=1, source_target_pairs={{0,4},{1,5},{2,6},{3,7},{4,0},{5,1},{6,2},{7,3},{8,12},{9,13},{10,... | collective-permute-start | bytes 835592 | tf_op jit(solution)/shard_map/ppermute | solution.py:938
  43.3 10.6 %collective-permute-start.15 = (f32[8,392,128]{2,1,0:T(8,128)S(1)}, f32[8,392,128]{2,1,0:T(8,128)S(1)}, u32[]{:S(2)}, u32[]{:S(2)}) collective-permute-start(f32[8,392,128]{2,1,0:T(8,128)S(1)} %shard_map.319.refs_6_), channel_id=1, source_target_pairs={{0,1},{1,0},{2,3},{3,2},{4,5},{5,4},{6,7},{7,6},{8,9},{9,8},{10,11... | collective-permute-start | bytes 4816904 | tf_op jit(solution)/shard_map/ppermute | solution.py:938
  47.7 35.8 %collective-permute-start.21 = (f32[8,392,128]{2,1,0:T(8,128)S(1)}, f32[8,392,128]{2,1,0:T(8,128)S(1)}, u32[]{:S(2)}, u32[]{:S(2)}) collective-permute-start(f32[8,392,128]{2,1,0:T(8,128)S(1)} %shard_map.318.refs_6_), channel_id=1, source_target_pairs={{0,1},{1,0},{2,3},{3,2},{4,5},{5,4},{6,7},{7,6},{8,9},{9,8},{10,11... | collective-permute-start | bytes 4816904 | tf_op jit(solution)/shard_map/ppermute | solution.py:938
  203.7 11.9 %collective-permute-start.49 = (f32[8,392,128]{2,1,0:T(8,128)S(1)}, f32[8,392,128]{2,1,0:T(8,128)S(1)}, u32[]{:S(2)}, u32[]{:S(2)}) collective-permute-start(f32[8,392,128]{2,1,0:T(8,128)S(1)} %get-tuple-element.242), channel_id=1, source_target_pairs={{0,1},{1,0},{2,3},{3,2},{4,5},{5,4},{6,7},{7,6},{8,9},{9,8},{10,11... | collective-permute-start | bytes 4816904 | tf_op jit(solution)/shard_map/ppermute | solution.py:938
  205.7 9.9 %collective-permute-start.50 = (f32[8,392,128]{2,1,0:T(8,128)S(1)}, f32[8,392,128]{2,1,0:T(8,128)S(1)}, u32[]{:S(2)}, u32[]{:S(2)}) collective-permute-start(f32[8,392,128]{2,1,0:T(8,128)S(1)} %get-tuple-element.250), channel_id=1, source_target_pairs={{0,1},{1,0},{2,3},{3,2},{4,5},{5,4},{6,7},{7,6},{8,9},{9,8},{10,11... | collective-permute-start | bytes 4816904 | tf_op jit(solution)/shard_map/ppermute | solution.py:938
  206.2 16.1 %collective-permute-start.52 = (f32[128,256]{1,0:T(8,128)S(1)}, f32[128,256]{1,0:T(8,128)S(1)}, u32[]{:S(2)}, u32[]{:S(2)}) collective-permute-start(f32[128,256]{1,0:T(8,128)S(1)} %copy-done.9), channel_id=1, source_target_pairs={{0,1},{1,2},{2,3},{4,5},{5,6},{6,7},{8,9},{9,10},{10,11},{12,13},{... | collective-permute-start | bytes 393224 | tf_op jit(solution)/shard_map/ppermute | solution.py:955
  208.2 14.1 %collective-permute-start.53 = (f32[128,256]{1,0:T(8,128)S(1)}, f32[128,256]{1,0:T(8,128)S(1)}, u32[]{:S(2)}, u32[]{:S(2)}) collective-permute-start(f32[128,256]{1,0:T(8,128)S(1)} %copy-done.8), channel_id=1, source_target_pairs={{1,0},{2,1},{3,2},{5,4},{6,5},{7,6},{9,8},{10,9},{11,10},{13,12},{... | collective-permute-start | bytes 393224 | tf_op jit(solution)/shard_map/ppermute | solution.py:955
  216.0 14.8 %collective-permute-start.51 = (f32[4,2,128,128]{3,2,1,0:T(8,128)S(1)}, f32[4,2,128,128]{3,2,1,0:T(8,128)S(1)}, u32[]{:S(2)}, u32[]{:S(2)}) collective-permute-start(f32[4,2,128,128]{3,2,1,0:T(8,128)S(1)} %get-tuple-element.254), channel_id=1, source_target_pairs={{0,8},{1,9},{2,10},{3,11},{4,12},{5,13},{6,14},{7,15},{8,0},{9,1},... | collective-permute-start | bytes 1572872 | tf_op jit(solution)/shard_map/ppermute | solution.py:938
  217.1 13.7 %collective-permute-start.54 = (f32[4,2,128,128]{3,2,1,0:T(8,128)S(1)}, f32[4,2,128,128]{3,2,1,0:T(8,128)S(1)}, u32[]{:S(2)}, u32[]{:S(2)}) collective-permute-start(f32[4,2,128,128]{3,2,1,0:T(8,128)S(1)} %get-tuple-element.260), channel_id=1, source_target_pairs={{0,4},{1,5},{2,6},{3,7},{4,0},{5,1},{6,2},{7,3},{8,12},{9,13},{10,... | collective-permute-start | bytes 1572872 | tf_op jit(solution)/shard_map/ppermute | solution.py:938
  218.1 16.5 %collective-permute-start.55 = (f32[4,2,136,128]{3,2,1,0:T(8,128)S(1)}, f32[4,2,136,128]{3,2,1,0:T(8,128)S(1)}, u32[]{:S(2)}, u32[]{:S(2)}) collective-permute-start(f32[4,2,136,128]{3,2,1,0:T(8,128)S(1)} %get-tuple-element.261), channel_id=1, source_target_pairs={{0,2},{1,3},{2,0},{3,1},{4,6},{5,7},{6,4},{7,5},{8,10},{9,11},{10,... | collective-permute-start | bytes 1671176 | tf_op jit(solution)/shard_map/ppermute | solution.py:938
  234.8 8.6 %collective-permute-start.56 = (f32[2,2,128,128]{3,2,1,0:T(8,128)S(1)}, f32[2,2,128,128]{3,2,1,0:T(8,128)S(1)}, u32[]{:S(2)}, u32[]{:S(2)}) collective-permute-start(f32[2,2,128,128]{3,2,1,0:T(8,128)S(1)} %get-tuple-element.262), channel_id=1, source_target_pairs={{0,4},{1,5},{2,6},{3,7},{4,0},{5,1},{6,2},{7,3},{8,12},{9,13},{10,... | collective-permute-start | bytes 786440 | tf_op jit(solution)/shard_map/ppermute | solution.py:938
  235.9 7.5 %collective-permute-start.57 = (f32[2,2,128,128]{3,2,1,0:T(8,128)S(1)}, f32[2,2,128,128]{3,2,1,0:T(8,128)S(1)}, u32[]{:S(2)}, u32[]{:S(2)}) collective-permute-start(f32[2,2,128,128]{3,2,1,0:T(8,128)S(1)} %get-tuple-element.277), channel_id=1, source_target_pairs={{0,2},{1,3},{2,0},{3,1},{4,6},{5,7},{6,4},{7,5},{8,10},{9,11},{10,... | collective-permute-start | bytes 786440 | tf_op jit(solution)/shard_map/ppermute | solution.py:938
  236.3 7.1 %collective-permute-start.58 = (f32[2,2,136,128]{3,2,1,0:T(8,128)S(1)}, f32[2,2,136,128]{3,2,1,0:T(8,128)S(1)}, u32[]{:S(2)}, u32[]{:S(2)}) collective-permute-start(f32[2,2,136,128]{3,2,1,0:T(8,128)S(1)} %get-tuple-element.278), channel_id=1, source_target_pairs={{0,8},{1,9},{2,10},{3,11},{4,12},{5,13},{6,14},{7,15},{8,0},{9,1},... | collective-permute-start | bytes 835592 | tf_op jit(solution)/shard_map/ppermute | solution.py:938
  243.6 7.6 %collective-permute-start.61 = (f32[1,2,136,128]{3,2,1,0:T(8,128)S(1)}, f32[1,2,136,128]{3,2,1,0:T(8,128)S(1)}, u32[]{:S(2)}, u32[]{:S(2)}) collective-permute-start(f32[1,2,136,128]{3,2,1,0:T(8,128)S(1)} %get-tuple-element.284), channel_id=1, source_target_pairs={{0,4},{1,5},{2,6},{3,7},{4,0},{5,1},{6,2},{7,3},{8,12},{9,13},{10,... | collective-permute-start | bytes 417800 | tf_op jit(solution)/shard_map/ppermute | solution.py:938
  251.8 8.9 %collective-permute-start.62 = (f32[392,128]{1,0:T(8,128)S(1)}, f32[392,128]{1,0:T(8,128)S(1)}, u32[]{:S(2)}, u32[]{:S(2)}) collective-permute-start(f32[392,128]{1,0:T(8,128)S(1)} %get-tuple-element.285), channel_id=1, source_target_pairs={{0,16},{1,17},{2,18},{3,19},{4,20},{5,21},{6,22},{7,23},{8,24},{9,... | collective-permute-start | bytes 602120 | tf_op jit(solution)/shard_map/ppermute | solution.py:938
  (51 other events, 183.6 us)
